TPU v7x, 256 devices: a whole 4x4x8 slice. The times are simulated.
256 devices in a mesh: context: 32 (over z, y), tensor: 8 (over x, core).
Axes of the slice: x: 4, y: 4, z: 8, core: 2. Of those that a mesh axis runs over, the one named last changes fastest.
Arguments:
- stream: bfloat16 [8192, 8192], P('context', 'tensor'), may hold values from -12.5 to 12.5
- pre_gates: bfloat16 [3, 8192, 8192], P(None, 'context', 'tensor'), may hold values from -4 to 4
- post_gates: bfloat16 [3, 8192, 8192], P(None, 'context', 'tensor'), may hold values from -4 to 4
- norm_gains: float32 [3, 8192], P(None, 'tensor'), may hold values from 0.1 to 1.9
- se_taps: float32 [7, 8192], P(None, 'tensor'), may hold values from -2 to 2
- mr_taps: float32 [128, 8192], P(None, 'tensor'), may hold values from -0.5 to 0.5
- li_residues: float32 [8192, 16], P('tensor'), may hold values from -1.5 to 1.5
- li_decays: float32 [8192, 16], P('tensor'), may hold values from 3.0517578e-05 to 0.05
- cotangent: bfloat16 [8192, 8192], P('context', 'tensor'), may hold values from -6 to 6
Outputs:
- layer_output: bfloat16 [8192, 8192], P('context', 'tensor')
- stream_grad: bfloat16 [8192, 8192], P('context', 'tensor')
All inputs are finite; a program needn't handle non-finite values.
Results may differ from a plain program's by a relative error of at most 0.017.
Values may be sent and summed in bfloat16 or wider, within the bound.
A program may use at most 128 MiB of HBM per device.

v0:
```python
import math

import jax
import jax.numpy as jnp
from jax import lax
from jax.sharding import PartitionSpec as P

D = 8192


epsilon = 1e-06


def from_behind(value, axis, by):
    size = lax.axis_size(axis)
    pairs = [(i, i + by) for i in range(size) if 0 <= i + by < size]
    return lax.ppermute(value, axis, pairs)


def depthwise(padded, kernel):
    result = lax.conv_general_dilated(
        padded[None],
        kernel[:, None, :],
        (1,),
        "VALID",
        dimension_numbers=("NWC", "WIO", "NWC"),
        feature_group_count=kernel.shape[1],
        precision=lax.Precision.HIGHEST,
    )
    return result[0]


def short_conv(signal, filter_taps, adjoint):
    rim_rows = filter_taps.shape[0] - 1
    if adjoint:
        edge_rows = signal[:rim_rows]
        offset = -1
    else:
        edge_rows = signal[signal.shape[0] - rim_rows :]
        offset = 1
    neighbour = from_behind(edge_rows, "context", offset)
    values = signal.astype(jnp.float32)
    rim_values = neighbour.astype(jnp.float32)
    if adjoint:
        return depthwise(jnp.concatenate([values, rim_values], axis=0), filter_taps)
    return depthwise(jnp.concatenate([rim_values, values], axis=0), filter_taps[::-1])


def filter_weights(li_residues, li_decays):
    return li_residues * jnp.sqrt(-jnp.expm1(-2.0 * li_decays))


def inverse_rms(values):
    totals = lax.psum(jnp.sum(values * values, axis=1, keepdims=True), "tensor")
    return lax.rsqrt(totals / D + epsilon)


def dft_table(points):
    indices = jnp.arange(points, dtype=jnp.int32)
    angle = (indices[:, None] * indices[None, :] % points).astype(jnp.float32) * (
        2.0 * math.pi / points
    )
    return (jnp.cos(angle), jnp.sin(angle))


def spectrum(signal, fourier):
    cos_first, sin_first, cos_second, sin_second, cos_twist, sin_twist = fourier
    half_rows = cos_first.shape[0] // 2
    signal_grid = signal.reshape(signal.shape[0], half_rows, cos_second.shape[0])
    highest = lax.Precision.HIGHEST
    section_re = jnp.einsum("kn,cnm->ckm", cos_first[:, :half_rows], signal_grid, precision=highest)
    section_im = -jnp.einsum(
        "kn,cnm->ckm", sin_first[:, :half_rows], signal_grid, precision=highest
    )
    turned_re = section_re * cos_twist + section_im * sin_twist
    turned_im = section_im * cos_twist - section_re * sin_twist
    out_re = jnp.einsum("ckm,mj->ckj", turned_re, cos_second, precision=highest) + jnp.einsum(
        "ckm,mj->ckj", turned_im, sin_second, precision=highest
    )
    out_im = jnp.einsum("ckm,mj->ckj", turned_im, cos_second, precision=highest) - jnp.einsum(
        "ckm,mj->ckj", turned_re, sin_second, precision=highest
    )
    return (out_re, out_im)


def inverse_spectrum(prod_re, prod_im, fourier):
    cos_first, sin_first, cos_second, sin_second, cos_twist, sin_twist = fourier
    half_rows = cos_first.shape[0] // 2
    length = cos_first.shape[0] * cos_second.shape[0]
    highest = lax.Precision.HIGHEST
    section_re = jnp.einsum("ckj,jm->ckm", prod_re, cos_second, precision=highest) - jnp.einsum(
        "ckj,jm->ckm", prod_im, sin_second, precision=highest
    )
    section_im = jnp.einsum("ckj,jm->ckm", prod_im, cos_second, precision=highest) + jnp.einsum(
        "ckj,jm->ckm", prod_re, sin_second, precision=highest
    )
    turned_re = section_re * cos_twist - section_im * sin_twist
    turned_im = section_im * cos_twist + section_re * sin_twist
    result = jnp.einsum(
        "nk,ckm->cnm", cos_first[:half_rows], turned_re, precision=highest
    ) - jnp.einsum("nk,ckm->cnm", sin_first[:half_rows], turned_im, precision=highest)
    return result.reshape(result.shape[0], -1) / length


def spectral_tables(weights_all, li_decays, tok_rows):
    groups = lax.axis_size("context")
    part_rows = weights_all.shape[0] // groups
    row_start = lax.axis_index("context") * part_rows
    weight_part = lax.dynamic_slice_in_dim(weights_all, row_start, part_rows, 0)
    rate_part = lax.dynamic_slice_in_dim(li_decays, row_start, part_rows, 0)
    positions = jnp.arange(tok_rows * groups, dtype=jnp.float32)
    decay_table = jnp.exp(-rate_part[:, :, None] * positions[None, None, :])
    kernel = jnp.einsum("cr,crt->ct", weight_part, decay_table, precision=lax.Precision.HIGHEST)
    first_len = tok_rows // 2
    second = 4 * groups
    length = first_len * second
    cos_first, sin_first = dft_table(first_len)
    cos_second, sin_second = dft_table(second)
    first_idx = jnp.arange(first_len, dtype=jnp.int32)
    second_idx = jnp.arange(second, dtype=jnp.int32)
    twist_angle = (first_idx[:, None] * second_idx[None, :] % length).astype(jnp.float32) * (
        2.0 * math.pi / length
    )
    fourier = (
        cos_first,
        sin_first,
        cos_second,
        sin_second,
        jnp.cos(twist_angle),
        jnp.sin(twist_angle),
    )
    kernel_re, kernel_im = spectrum(kernel, fourier)
    return (fourier, kernel_re, kernel_im)


def spectral_apply(signal, fourier, kernel_re, kernel_im, adjoint):
    columns = lax.all_to_all(signal.T, "context", split_axis=0, concat_axis=1, tiled=True)
    signal_re, signal_im = spectrum(columns.astype(jnp.float32), fourier)
    if adjoint:
        prod_re = signal_re * kernel_re + signal_im * kernel_im
        prod_im = signal_im * kernel_re - signal_re * kernel_im
    else:
        prod_re = signal_re * kernel_re - signal_im * kernel_im
        prod_im = signal_re * kernel_im + signal_im * kernel_re
    result = inverse_spectrum(prod_re, prod_im, fourier).astype(jnp.bfloat16)
    restored = lax.all_to_all(result, "context", split_axis=1, concat_axis=0, tiled=True)
    return restored.T.astype(jnp.float32)


def per_device(
    stream, pre_gates, post_gates, norm_gains, se_taps, mr_taps, li_residues, li_decays, cotangent
):
    kernels = (se_taps, mr_taps)
    tok_rows = stream.shape[0]
    weights_all = filter_weights(li_residues, li_decays)
    fourier, kernel_re, kernel_im = spectral_tables(weights_all, li_decays, tok_rows)

    def long_apply(signal, adjoint):
        return spectral_apply(signal, fourier, kernel_re, kernel_im, adjoint)

    history = []
    current = stream
    for layer in range(3):
        values = current.astype(jnp.float32)
        norm_scale = inverse_rms(values)
        mixed = (
            pre_gates[layer].astype(jnp.float32) * values * norm_scale * norm_gains[layer]
        ).astype(jnp.bfloat16)
        if layer < 2:
            conv_out = short_conv(mixed, kernels[layer], False)
        else:
            conv_out = lax.optimization_barrier(
                long_apply(mixed, False).astype(jnp.bfloat16)
            ).astype(jnp.float32)
        history.append((values, norm_scale))
        current = (values + post_gates[layer].astype(jnp.float32) * conv_out).astype(jnp.bfloat16)
    gradient = cotangent
    for layer in (2, 1, 0):
        values, norm_scale = history[layer]
        gated_back = (post_gates[layer].astype(jnp.float32) * gradient.astype(jnp.float32)).astype(
            jnp.bfloat16
        )
        if layer < 2:
            spread = short_conv(gated_back, kernels[layer], True)
        else:
            spread = lax.optimization_barrier(
                long_apply(gated_back, True).astype(jnp.bfloat16)
            ).astype(jnp.float32)
        upstream = spread * pre_gates[layer].astype(jnp.float32) * norm_gains[layer]
        normed = values * norm_scale
        projection = lax.psum(jnp.sum(upstream * normed, axis=1, keepdims=True), "tensor") / D
        gradient = (
            gradient.astype(jnp.float32) + (upstream - normed * projection) * norm_scale
        ).astype(jnp.bfloat16)
    return (current, gradient)


def solution(mesh):
    placed = (
        P("context", "tensor"),
        P(None, "context", "tensor"),
        P(None, "context", "tensor"),
        P(None, "tensor"),
        P(None, "tensor"),
        P(None, "tensor"),
        P("tensor", None),
        P("tensor", None),
        P("context", "tensor"),
    )
    return jax.shard_map(
        per_device,
        mesh=mesh,
        in_specs=placed,
        out_specs=(P("context", "tensor"), P("context", "tensor")),
        check_vma=False,
    )
```

profile of v0, /device:TPU:25, one launch (start us, length us, event | category | flops | bytes accessed | tf_op | source)
XLA Modules:
  0.0 359.3 jit_solution(14064065432497670732)
XLA Ops:
  2.7 12.4 %psum.42 = f32[256,1]{0,1:T(1,128)S(1)} all-reduce(f32[256,1]{0,1:T(1,128)S(1)} %bitcast.316), channel_id=1, replica_groups=mesh['context'=32,'tensor'=8] {'tensor'}, use_global_device_ids=true, to_apply=%region_1.2 | all-reduce | flops 256 | bytes 2048 | tf_op jit(solution)/shard_map/psum | solution.py:54
  21.6 11.0 %fusion = f32[32,1,8192]{2,1,0:T(1,128)S(1)} fusion(f32[32,16,1]{1,2,0:T(1,128)S(1)} %copy.144, f32[32,16]{1,0:T(8,128)S(1)} %copy.83), kind=kOutput, calls=%fused_computation | convolution fusion | flops 54525952 | bytes 1052672 | tf_op jit(solution)/shard_map/cr,crt->ct/dot_general | solution.py:113
  44.1 5.6 %convolution_add_fusion.3 = f32[32,128,128]{2,1,0:T(8,128)} fusion(f32[32,128,128]{2,1,0:T(8,128)S(1)} %fusion.130, f32[32,128,128]{2,1,0:T(8,128)S(1)} %fusion.202, f32[32,128,128]{2,1,0:T(8,128)S(1)} %fusion.205, f32[128,128]{0,1:T(8,128)S(1)} %get-tuple-element.23, f32[128,128]{0,1:T(8,128)S(1)} %get-tuple-element.24), kind=kOutput, calls=%fused_computation.63 | convolution fusion | flops 808157184 | bytes 8519680 | tf_op jit(solution)/shard_map/ckm,mj->ckj/dot_general | solution.py:77
  49.7 5.0 %fusion.126 = f32[32,128,128]{2,1,0:T(8,128)} fusion(f32[32,128,128]{2,1,0:T(8,128)S(1)} %fusion.202, f32[32,128,128]{2,1,0:T(8,128)S(1)} %fusion.205, f32[128,128]{0,1:T(8,128)S(1)} %get-tuple-element.23, f32[128,128]{0,1:T(8,128)S(1)} %get-tuple-element.24), kind=kOutput, calls=%fused_computation.164 | convolution fusion | flops 807632896 | bytes 6422528 | tf_op jit(solution)/shard_map/ckm,mj->ckj/dot_general | solution.py:80
  69.8 14.9 %psum.43 = f32[256,1]{0,1:T(1,128)S(1)} all-reduce(f32[256,1]{0,1:T(1,128)S(1)} %bitcast.314), channel_id=1, replica_groups=mesh['context'=32,'tensor'=8] {'tensor'}, use_global_device_ids=true, to_apply=%region_3.4 | all-reduce | flops 256 | bytes 2048 | tf_op jit(solution)/shard_map/psum | solution.py:54
  90.9 6.4 %convolution_subtract_fusion.3 = f32[32,128,128]{2,1,0:T(8,128)} fusion(f32[32,128,128]{2,1,0:T(8,128)} %fusion.126, f32[32,128,128]{2,1,0:T(8,128)S(1)} %fusion.202, f32[32,128,128]{2,1,0:T(8,128)S(1)} %copy-done.1, f32[128,128]{0,1:T(8,128)S(1)} %get-tuple-element.23, f32[128,128]{0,1:T(8,128)S(1)} %get-tuple-element.24), kind=kOutput, calls=%fused_computation.61 | convolution fusion | flops 808157184 | bytes 8519680 | tf_op jit(solution)/shard_map/ckm,mj->ckj/dot_general | solution.py:80
  99.3 9.8 %all-to-all-start.2 = ((bf16[32,32,256]{2,1,0:T(8,128)(2,1)}), bf16[32,32,256]{2,1,0:T(8,128)(2,1)S(1)}, u32[]{:S(2)}, u32[]{:S(2)}) async-start(bf16[32,32,256]{2,1,0:T(8,128)(2,1)} %bitcast.52), calls=%async_computation.2 | async-start | bytes 1048576 | tf_op jit(solution)/shard_map/all_to_all | solution.py:137
  110.3 11.4 %fusion.29 = f32[1,256,1024]{2,0,1:T(1,128)S(1)} fusion(bf16[1,383,1024]{2,1,0:T(8,128)(2,1)S(1)} %maximum_bitcast_fusion, f32[128,1,1024]{2,0,1:T(8,128)} %bitcast.289), kind=kOutput, calls=%fused_computation.67 | convolution fusion | flops 402653184 | bytes 2357248 | tf_op jit(solution)/shard_map/conv_general_dilated | solution.py:21
  123.1 13.3 %psum.44 = f32[256,1]{0,1:T(1,128)S(1)} all-reduce(f32[256,1]{0,1:T(1,128)S(1)} %bitcast.315), channel_id=1, replica_groups=mesh['context'=32,'tensor'=8] {'tensor'}, use_global_device_ids=true, to_apply=%region_5.6 | all-reduce | flops 256 | bytes 2048 | tf_op jit(solution)/shard_map/psum | solution.py:54
  138.6 9.4 %all-to-all-start = ((bf16[32,32,256]{2,1,0:T(8,128)(2,1)}), bf16[32,32,256]{2,1,0:T(8,128)(2,1)}, u32[]{:S(2)}, u32[]{:S(2)}) async-start(bf16[32,32,256]{2,1,0:T(8,128)(2,1)} %bitcast.22), calls=%async_computation | async-start | bytes 1048576 | tf_op jit(solution)/shard_map/all_to_all | solution.py:137
  156.8 5.0 %fusion.136 = f32[32,128,128]{2,1,0:T(8,128)} fusion(f32[32,128,128]{2,1,0:T(8,128)S(1)} %fusion.201, f32[32,128,128]{2,1,0:T(8,128)S(1)} %fusion.204, f32[128,128]{0,1:T(8,128)S(1)} %get-tuple-element.23, f32[128,128]{0,1:T(8,128)S(1)} %get-tuple-element.24), kind=kOutput, calls=%fused_computation.167 | convolution fusion | flops 807632896 | bytes 6422528 | tf_op jit(solution)/shard_map/ckm,mj->ckj/dot_general | solution.py:77
  161.8 5.4 %convolution_subtract_fusion.1 = f32[32,128,128]{2,1,0:T(8,128)} fusion(f32[32,128,128]{2,1,0:T(8,128)S(1)} %fusion.132, f32[32,128,128]{2,1,0:T(8,128)S(1)} %fusion.201, f32[32,128,128]{2,1,0:T(8,128)S(1)} %fusion.204, f32[128,128]{0,1:T(8,128)S(1)} %get-tuple-element.23, f32[128,128]{0,1:T(8,128)S(1)} %get-tuple-element.24), kind=kOutput, calls=%fused_computation.57 | convolution fusion | flops 808157184 | bytes 8519680 | tf_op jit(solution)/shard_map/ckm,mj->ckj/dot_general | solution.py:80
  178.8 4.2 %fusion.120 = f32[32,128,128]{2,1,0:T(8,128)S(1)} fusion(f32[32,128,128]{2,1,0:T(8,128)S(1)} %fusion.203, f32[32,128,128]{2,1,0:T(8,128)S(1)} %fusion.206, f32[128,128]{0,1:T(8,128)S(1)} %get-tuple-element.23, f32[128,128]{0,1:T(8,128)S(1)} %get-tuple-element.24), kind=kOutput, calls=%fused_computation.162 | convolution fusion | flops 807632896 | bytes 6422528 | tf_op jit(solution)/shard_map/ckm,mj->ckj/dot_general | solution.py:80
  186.9 3.9 %convolution_subtract_fusion.4 = f32[32,128,128]{2,1,0:T(8,128)S(1)} fusion(f32[32,128,128]{2,1,0:T(8,128)S(1)} %fusion.120, f32[32,128,128]{2,1,0:T(8,128)S(1)} %fusion.203, f32[32,128,128]{2,1,0:T(8,128)S(1)} %fusion.206, f32[128,128]{0,1:T(8,128)S(1)} %get-tuple-element.23, f32[128,128]{0,1:T(8,128)S(1)} %get-tuple-element.24), kind=kOutput, calls=%fused_computation.62 | convolution fusion | flops 808157184 | bytes 8519680 | tf_op jit(solution)/shard_map/ckm,mj->ckj/dot_general | solution.py:80
  190.8 6.2 %multiply_subtract_fusion = (f32[32,128,128]{2,1,0:T(8,128)}, f32[32,128,128]{2,1,0:T(8,128)}, f32[32,128,128]{2,1,0:T(8,128)S(1)}, f32[32,128,128]{2,1,0:T(8,128)S(1)}) fusion(f32[32,128,128]{2,1,0:T(8,128)S(1)} %copy-done.10, f32[32,128,128]{2,1,0:T(8,128)S(1)} %copy-done.11, f32[32,128,128]{2,1,0:T(8,128)S(1)} %copy-done.9, ...), kind=kOutput, calls=%fused_computation.31 | convolution fusion | flops 814448640 | bytes 25296896 | tf_op jit(solution)/shard_map/ckm,mj->ckj/dot_general | solution.py:77
  216.7 9.3 %all-to-all-start.1 = ((bf16[32,32,256]{2,0,1:T(8,128)(2,1)}), bf16[32,32,256]{2,0,1:T(8,128)(2,1)}, u32[]{:S(2)}, u32[]{:S(2)}) async-start(bf16[32,32,256]{2,0,1:T(8,128)(2,1)} %copy.108), calls=%async_computation.1 | async-start | bytes 1048576 | tf_op jit(solution)/shard_map/all_to_all | solution.py:146
  243.8 9.3 %all-to-all-start.3 = ((bf16[32,32,256]{2,0,1:T(8,128)(2,1)}), bf16[32,32,256]{2,0,1:T(8,128)(2,1)}, u32[]{:S(2)}, u32[]{:S(2)}) async-start(bf16[32,32,256]{2,0,1:T(8,128)(2,1)} %copy.132), calls=%async_computation.3 | async-start | bytes 1048576 | tf_op jit(solution)/shard_map/all_to_all | solution.py:146
  255.2 12.7 %all-to-all-done.3 = bf16[32,32,256]{2,0,1:T(8,128)(2,1)} async-done(((bf16[32,32,256]{2,0,1:T(8,128)(2,1)}), bf16[32,32,256]{2,0,1:T(8,128)(2,1)}, u32[]{:S(2)}, u32[]{:S(2)}) %all-to-all-start.3) | async-done | bytes 524320 | tf_op jit(solution)/shard_map/all_to_all | solution.py:146
  271.4 15.1 %psum.45 = f32[256,1]{0,1:T(1,128)S(1)} all-reduce(f32[256,1]{0,1:T(1,128)S(1)} %bitcast.317), channel_id=1, replica_groups=mesh['context'=32,'tensor'=8] {'tensor'}, use_global_device_ids=true, to_apply=%region_7.8 | all-reduce | flops 256 | bytes 2048 | tf_op jit(solution)/shard_map/psum | solution.py:191
  292.4 8.7 %collective-permute-done.2 = bf16[127,1024]{1,0:T(8,128)(2,1)S(1)} collective-permute-done((bf16[127,1024]{1,0:T(8,128)(2,1)S(1)}, bf16[127,1024]{1,0:T(8,128)(2,1)S(1)}, u32[]{:S(2)}, u32[]{:S(2)}) %collective-permute-start.2) | collective-permute-done | bytes 260128 | tf_op jit(solution)/shard_map/ppermute | solution.py:17
  301.2 10.8 %fusion.27 = f32[1,256,1024]{2,0,1:T(1,128)S(1)} fusion(bf16[1,383,1024]{2,1,0:T(8,128)(2,1)S(1)} %maximum_bitcast_fusion.1, f32[128,1,1024]{2,0,1:T(8,128)S(1)} %bitcast.288), kind=kOutput, calls=%fused_computation.65 | convolution fusion | flops 402653184 | bytes 2357248 | tf_op jit(solution)/shard_map/conv_general_dilated | solution.py:21
  313.3 13.3 %psum.46 = f32[256,1]{0,1:T(1,128)S(1)} all-reduce(f32[256,1]{0,1:T(1,128)S(1)} %bitcast.310), channel_id=1, replica_groups=mesh['context'=32,'tensor'=8] {'tensor'}, use_global_device_ids=true, to_apply=%region_9.10 | all-reduce | flops 256 | bytes 2048 | tf_op jit(solution)/shard_map/psum | solution.py:191
  331.3 4.7 %collective-permute-done.3 = bf16[6,1024]{1,0:T(8,128)(2,1)S(1)} collective-permute-done((bf16[6,1024]{1,0:T(8,128)(2,1)S(1)}, bf16[6,1024]{1,0:T(8,128)(2,1)S(1)}, u32[]{:S(2)}, u32[]{:S(2)}) %collective-permute-start.3) | collective-permute-done | bytes 12320 | tf_op jit(solution)/shard_map/ppermute | solution.py:17
  342.9 13.6 %psum.47 = f32[256,1]{0,1:T(1,128)S(1)} all-reduce(f32[256,1]{0,1:T(1,128)S(1)} %bitcast.311), channel_id=1, replica_groups=mesh['context'=32,'tensor'=8] {'tensor'}, use_global_device_ids=true, to_apply=%region_11.12 | all-reduce | flops 256 | bytes 2048 | tf_op jit(solution)/shard_map/psum | solution.py:191
  (144 shorter events, 136.2 us)
Async XLA Ops:
  16.6 41.0 %collective-permute-start = (bf16[6,1024]{1,0:T(8,128)(2,1)S(1)}, bf16[6,1024]{1,0:T(8,128)(2,1)S(1)}, u32[]{:S(2)}, u32[]{:S(2)}) collective-permute-start(bf16[6,1024]{1,0:T(8,128)(2,1)S(1)} %slice.99), channel_id=1, source_target_pairs={{0,8},{8,16},{16,24},{24,32},{32,40},{40,48},{48,56},{56,64},{64,7... | collective-permute-start | bytes 36872 | tf_op jit(solution)/shard_map/ppermute | solution.py:17
  40.3 9.4 %copy-start = (f32[32,128,128]{2,1,0:T(8,128)}, f32[32,128,128]{2,1,0:T(8,128)S(1)}, u32[]{:S(2)}) copy-start(f32[32,128,128]{2,1,0:T(8,128)S(1)} %fusion.205) | copy-start | bytes 6291460
  49.7 5.1 %copy-start.23 = (f32[7,1024]{1,0:T(8,128)S(1)}, f32[7,1024]{1,0:T(8,128)}, u32[]{:S(2)}) copy-start(f32[7,1024]{1,0:T(8,128)} %param.13) | copy-start | bytes 86020
  49.7 5.2 %copy-start.21 = (f32[128,1024]{1,0:T(8,128)S(1)}, f32[128,1024]{1,0:T(8,128)}, u32[]{:S(2)}) copy-start(f32[128,1024]{1,0:T(8,128)} %param.14) | copy-start | bytes 1572868
  57.8 4.3 %copy-start.24 = (pred[8,33]{0,1:T(8,128)(4,1)S(1)}, pred[8,33]{0,1:T(8,128)(4,1)}, u32[]{:S(2)}) copy-start(pred[8,33]{0,1:T(8,128)(4,1)} %constant.78) | copy-start | bytes 796
  62.7 4.3 %copy-start.7 = (bf16[256,1024]{1,0:T(8,128)(2,1)S(1)}, bf16[256,1024]{1,0:T(8,128)(2,1)}, u32[]{:S(2)}) copy-start(bf16[256,1024]{1,0:T(8,128)(2,1)} %param.9) | copy-start | bytes 1572868
  84.7 6.2 %copy-start.1 = (f32[32,128,128]{2,1,0:T(8,128)S(1)}, f32[32,128,128]{2,1,0:T(8,128)}, u32[]{:S(2)}) copy-start(f32[32,128,128]{2,1,0:T(8,128)} %copy-done) | copy-start | bytes 6291460
  87.7 21.5 %collective-permute-start.1 = (bf16[127,1024]{1,0:T(8,128)(2,1)}, bf16[127,1024]{1,0:T(8,128)(2,1)}, u32[]{:S(2)}, u32[]{:S(2)}) collective-permute-start(bf16[127,1024]{1,0:T(8,128)(2,1)} %slice.102), channel_id=1, source_target_pairs={{0,8},{8,16},{16,24},{24,32},{32,40},{40,48},{48,56},{56,64},{64,7... | collective-permute-start | bytes 780296 | tf_op jit(solution)/shard_map/ppermute | solution.py:17
  97.2 12.0 %copy-start.18 = (bf16[256,1024]{1,0:T(8,128)(2,1)S(1)}, bf16[256,1024]{1,0:T(8,128)(2,1)}, u32[]{:S(2)}) copy-start(bf16[256,1024]{1,0:T(8,128)(2,1)} %copy-done.17) | copy-start | bytes 1572868
  99.3 39.3 %all-to-all-start.2 = ((bf16[32,32,256]{2,1,0:T(8,128)(2,1)}), bf16[32,32,256]{2,1,0:T(8,128)(2,1)S(1)}, u32[]{:S(2)}, u32[]{:S(2)}) async-start(bf16[32,32,256]{2,1,0:T(8,128)(2,1)} %bitcast.52), calls=%async_computation.2 | async-start | bytes 1048576 | tf_op jit(solution)/shard_map/all_to_all | solution.py:137
  123.1 25.3 %copy-start.12 = (bf16[256,1024]{1,0:T(8,128)(2,1)}, bf16[256,1024]{1,0:T(8,128)(2,1)S(1)}, u32[]{:S(2)}) copy-start(bf16[256,1024]{1,0:T(8,128)(2,1)S(1)} %get-tuple-element.7) | copy-start | bytes 1572868
  138.6 28.6 %all-to-all-start = ((bf16[32,32,256]{2,1,0:T(8,128)(2,1)}), bf16[32,32,256]{2,1,0:T(8,128)(2,1)}, u32[]{:S(2)}, u32[]{:S(2)}) async-start(bf16[32,32,256]{2,1,0:T(8,128)(2,1)} %bitcast.22), calls=%async_computation | async-start | bytes 1048576 | tf_op jit(solution)/shard_map/all_to_all | solution.py:137
  152.9 8.9 %copy-start.2 = (f32[32,128,128]{2,1,0:T(8,128)}, f32[32,128,128]{2,1,0:T(8,128)S(1)}, u32[]{:S(2)}) copy-start(f32[32,128,128]{2,1,0:T(8,128)S(1)} %fusion.204) | copy-start | bytes 6291460
  183.0 7.8 %copy-start.11 = (f32[32,128,128]{2,1,0:T(8,128)S(1)}, f32[32,128,128]{2,1,0:T(8,128)}, u32[]{:S(2)}) copy-start(f32[32,128,128]{2,1,0:T(8,128)} %convolution_subtract_fusion.1) | copy-start | bytes 6291460
  212.4 13.6 %copy-start.4 = (f32[32,128,128]{2,1,0:T(8,128)S(1)}, f32[32,128,128]{2,1,0:T(8,128)}, u32[]{:S(2)}) copy-start(f32[32,128,128]{2,1,0:T(8,128)} %get-tuple-element.10) | copy-start | bytes 6291460
  216.7 27.1 %all-to-all-start.1 = ((bf16[32,32,256]{2,0,1:T(8,128)(2,1)}), bf16[32,32,256]{2,0,1:T(8,128)(2,1)}, u32[]{:S(2)}, u32[]{:S(2)}) async-start(bf16[32,32,256]{2,0,1:T(8,128)(2,1)} %copy.108), calls=%async_computation.1 | async-start | bytes 1048576 | tf_op jit(solution)/shard_map/all_to_all | solution.py:146
  241.5 28.4 %copy-start.6 = (bf16[3,256,1024]{2,1,0:T(8,128)(2,1)S(1)}, bf16[3,256,1024]{2,1,0:T(8,128)(2,1)}, u32[]{:S(2)}) copy-start(bf16[3,256,1024]{2,1,0:T(8,128)(2,1)} %param.10) | copy-start | bytes 4718596
  241.5 28.4 %copy-start.13 = (bf16[256,1024]{1,0:T(8,128)(2,1)S(1)}, bf16[256,1024]{1,0:T(8,128)(2,1)}, u32[]{:S(2)}) copy-start(bf16[256,1024]{1,0:T(8,128)(2,1)} %copy-done.12) | copy-start | bytes 1572868
  243.8 24.1 %all-to-all-start.3 = ((bf16[32,32,256]{2,0,1:T(8,128)(2,1)}), bf16[32,32,256]{2,0,1:T(8,128)(2,1)}, u32[]{:S(2)}, u32[]{:S(2)}) async-start(bf16[32,32,256]{2,0,1:T(8,128)(2,1)} %copy.132), calls=%async_computation.3 | async-start | bytes 1048576 | tf_op jit(solution)/shard_map/all_to_all | solution.py:146
  289.8 11.4 %copy-start.22 = (f32[128,1024]{1,0:T(8,128)S(1)}, f32[128,1024]{1,0:T(8,128)}, u32[]{:S(2)}) copy-start(f32[128,1024]{1,0:T(8,128)} %param.14) | copy-start | bytes 1572868
  289.8 11.3 %collective-permute-start.2 = (bf16[127,1024]{1,0:T(8,128)(2,1)S(1)}, bf16[127,1024]{1,0:T(8,128)(2,1)S(1)}, u32[]{:S(2)}, u32[]{:S(2)}) collective-permute-start(bf16[127,1024]{1,0:T(8,128)(2,1)S(1)} %slice.107), channel_id=1, source_target_pairs={{8,0},{16,8},{24,16},{32,24},{40,32},{48,40},{56,48},{64,56},{72,6... | collective-permute-start | bytes 780296 | tf_op jit(solution)/shard_map/ppermute | solution.py:17
  312.9 13.7 %copy-start.20 = (bf16[256,1024]{1,0:T(8,128)(2,1)S(1)}, bf16[256,1024]{1,0:T(8,128)(2,1)}, u32[]{:S(2)}) copy-start(bf16[256,1024]{1,0:T(8,128)(2,1)} %get-tuple-element.5) | copy-start | bytes 1572868
  329.3 6.6 %collective-permute-start.3 = (bf16[6,1024]{1,0:T(8,128)(2,1)S(1)}, bf16[6,1024]{1,0:T(8,128)(2,1)S(1)}, u32[]{:S(2)}, u32[]{:S(2)}) collective-permute-start(bf16[6,1024]{1,0:T(8,128)(2,1)S(1)} %slice.108), channel_id=1, source_target_pairs={{8,0},{16,8},{24,16},{32,24},{40,32},{48,40},{56,48},{64,56},{72,6... | collective-permute-start | bytes 36872 | tf_op jit(solution)/shard_map/ppermute | solution.py:17
  338.9 17.6 %copy-start.19 = (bf16[256,1024]{1,0:T(8,128)(2,1)S(1)}, bf16[256,1024]{1,0:T(8,128)(2,1)}, u32[]{:S(2)}) copy-start(bf16[256,1024]{1,0:T(8,128)(2,1)} %get-tuple-element.3) | copy-start | bytes 1572868
  (9 other events, 24.4 us)
where the time goes:
time: 367 us; the launch traced here: 359 us
  matrix products  135 us (37%)
  blocking collectives  82.5 us (22%)
  starting transfers between devices  48.8 us (13%)
  local copies, waits for them, and re-layouts  40.8 us (11%)
  waiting for transfers between devices  26.1 us (7%)
  other arithmetic  24.3 us (7%)
    psum x3, blocking collectives, per_device(): lax.psum(jnp.sum(upstream * normed, axis=1, keepdims=True), 'tensor') / D  41.9 us
    psum x3, blocking collectives, inverse_rms(): totals = lax.psum(jnp.sum(values * values, axis=1, keepdims=True), 'tensor')  40.6 us
    conv_general_dilated x4, matrix products, depthwise(): lax.conv_general_dilated(padded[None], kernel[:, None, :], (1,), 'VALID',...  23.3 us
    all_to_all x2, starting transfers between devices, spectral_apply(): lax.all_to_all(signal.T, 'context', split_axis=0, concat_axis=1, tiled=True)  19.3 us
    all_to_all x2, starting transfers between devices, spectral_apply(): lax.all_to_all(result, 'context', split_axis=1, concat_axis=0, tiled=True)  18.6 us
    dot_general x3, matrix products, spectrum(): jnp.einsum('ckm,mj->ckj', turned_im, sin_second, precision=highest)  15.7 us
    dot_general x3, matrix products, spectrum(): jnp.einsum('ckm,mj->ckj', turned_re, sin_second, precision=highest)  15.6 us
    ppermute x4, waiting for transfers between devices, from_behind(): return lax.ppermute(value, axis, pairs)  13.4 us
  transfers between devices with their start and end apart: 8, of which 3 were waited for; matrix products, arithmetic and copies ran while one was open for 28% of the time, Pallas kernels for 0%

commit v1 on v0

v1 whole, which is shorter than its diff:
```python
import functools
import math

import jax
import jax.numpy as jnp
import numpy as np
from jax import lax
from jax.experimental import pallas as pl
from jax.experimental.pallas import tpu as pltpu
from jax.sharding import PartitionSpec as P

EPSILON = 1e-06
F32 = jnp.float32
BF16 = jnp.bfloat16
MESH = pl.DeviceIdType.MESH
ROWS = 256
HALF = 128
LANE = 128
WIDE = 256
POLES = 16
YN = 4


def dft_matrix(points, used):
    freqs = (2 * np.arange(points // 2)[:, None] + 1) * np.arange(used)[None, :] % (2 * points)
    angle = freqs * (math.pi / points)
    return np.concatenate([np.cos(angle), -np.sin(angle)], axis=0)


def lanes(index, width=LANE):
    return pl.ds(pl.multiple_of(index * width, width), width)


def dot(a, b):
    return jnp.dot(a, b, preferred_element_type=F32)


def split(value):
    high = value.astype(BF16)
    return high, (value - high.astype(F32)).astype(BF16)


def kernel(
    zn,
    tn,
    channels,
    stream_h, pre_h, post_h, gains_h, se_h, mr_h, res_h, dec_h, cot_h, w1_h, v1_h, w2_h, v2_h,
    out_h, grad_h,
    x0, pre, post, gains, se, mr, res, dec, cot, w1, v1, w2, v2,
    x1, x2, a0, e0, a1, e1, e2, a2, u0, u1, u2, g1, g2, local, out, grad,
    dect, weight, decb, pow8, taps, h1, h2,
    sums, sums2, col_s, col_k, psa, psb,
    st_b, st_f, r1_b, r1_f, tz_b, tz_f, r2_b, r2_f, o3_b, o3_f, r3_b, r3_f,
    load_sem, store_sem, ps_send, ps_recv, halo_send, halo_recv,
    sc1_send, sc1_recv, sc2_send, sc2_recv, sc3_send, sc3_recv,
):
    k = lax.axis_index("context")
    me = lax.axis_index("tensor")
    kn = zn * YN
    z = k // YN
    y = k % YN
    width = x0.shape[1]
    tiles = width // LANE
    chunks = width // WIDE
    following = (k + 1) % kn
    preceding = (k + kn - 1) % kn

    plan = [
        (stream_h, x0), (dec_h, dec), (res_h, res), (cot_h, cot), (post_h.at[2], post.at[2]),
        (w1_h, w1), (mr_h, mr), (gains_h, gains), (se_h, se), (w2_h, w2), (v2_h, v2), (v1_h, v1),
        (pre_h.at[0], pre.at[0]), (post_h.at[0], post.at[0]), (pre_h.at[1], pre.at[1]),
        (post_h.at[1], post.at[1]), (pre_h.at[2], pre.at[2]),
    ]
    loads = [pltpu.make_async_copy(s, d, load_sem.at[i]) for i, (s, d) in enumerate(plan)]
    for load in loads:
        load.start()

    r2_b[...] = jnp.zeros_like(r2_b)
    r2_f[...] = jnp.zeros_like(r2_f)

    barrier = pltpu.get_barrier_semaphore()
    partners = [{"tensor": (me + d) % tn} for d in range(1, tn)]
    partners += [{"context": z * YN + (y + d) % YN} for d in range(1, YN)]
    partners += [{"context": ((z + d) % zn) * YN + y} for d in range(1, zn)]
    partners += [{"context": following}, {"context": preceding}]
    for partner in partners:
        pl.semaphore_signal(barrier, inc=1, device_id=partner, device_id_type=MESH)

    def row_of(total):
        return jnp.sum(total.T, axis=0, keepdims=True)

    def col_of(row):
        return jnp.broadcast_to(row, (LANE, ROWS)).T

    def exchange(slots, phase):
        sent = []
        for d in range(1, tn):
            sent.append(
                pltpu.make_async_remote_copy(
                    src_ref=slots.at[me],
                    dst_ref=slots.at[me],
                    send_sem=ps_send.at[phase, d],
                    recv_sem=ps_recv.at[phase, d],
                    device_id={"tensor": (me + d) % tn},
                    device_id_type=MESH,
                )
            )
        return sent

    def collect(sent, slots):
        for copy in sent:
            copy.wait_send()
        for copy in sent:
            copy.wait_recv()
        total = slots[0]
        for index in range(1, tn):
            total = total + slots[index]
        return total

    def halo(src, dst, index, target):
        return pltpu.make_async_remote_copy(
            src_ref=src,
            dst_ref=dst,
            send_sem=halo_send.at[index],
            recv_sem=halo_recv.at[index],
            device_id={"context": target},
            device_id_type=MESH,
        )

    def pole_tables():
        for part in range(tiles):
            here = slice(part * LANE, (part + 1) * LANE)
            dect[:, here] = dec[here, :].T
            weight[:, here] = res[here, :].T
        rate = dect[...]
        square = rate * rate
        series = rate * (
            1.0 + square * (1.0 / 6.0) * (1.0 + square * (1.0 / 20.0) * (1.0 + square * (1.0 / 42.0)))
        )
        weight[...] = weight[...] * jnp.sqrt(2.0 * jnp.exp(-rate) * series)
        for r in range(POLES):
            wide = jnp.broadcast_to(dect[r : r + 1, :], (8, width))
            decb[r] = wide
            pow8[r] = jnp.exp(-8.0 * wide)

    def sublane():
        return lax.broadcasted_iota(jnp.int32, (1, 8, LANE), 1).astype(F32)

    def states(src, dst, reverse):
        def quarter(q, carry):
            for side in range(2):
                where = lanes(q * 2 + side)
                base = pow8[:, :, where]
                total = jnp.zeros((POLES, 8, LANE), F32)

                def step(g, total):
                    group = (ROWS // 16 - 1 - g) if reverse else g
                    rows = pl.ds(pl.multiple_of(group * 16, 16), 16)
                    value = src[rows, where].astype(F32)
                    first, second = (value[8:], value[:8]) if reverse else (value[:8], value[8:])
                    total = total * base + first[None]
                    return total * base + second[None]

                total = lax.fori_loop(0, ROWS // 16, step, total)
                place = sublane() if reverse else 7.0 - sublane()
                total = total * jnp.exp(-decb[:, :, where] * place)
                dst[q, :, side * LANE : (side + 1) * LANE] = jnp.sum(total, axis=1)
            return carry

        lax.fori_loop(0, chunks, quarter, 0)

    def spread_poles(start, base, reverse, sink):
        def step(g, state):
            group = (ROWS // 16 - 1 - g) if reverse else g
            rows = pl.ds(pl.multiple_of(group * 16, 16), 16)
            first = jnp.sum(state, axis=0)
            state = state * base
            second = jnp.sum(state, axis=0)
            state = state * base
            pair = [second, first] if reverse else [first, second]
            sink(rows, jnp.concatenate(pair, axis=0))
            return state

        lax.fori_loop(0, ROWS // 16, step, start)

    def stacked(ref, index, where):
        return jnp.stack(
            [jnp.broadcast_to(ref[index, r : r + 1, where], (8, LANE)) for r in range(POLES)]
        )

    def stacked_flat(ref, where):
        return jnp.stack(
            [jnp.broadcast_to(ref[r : r + 1, where], (8, LANE)) for r in range(POLES)]
        )

    def filter_head():
        def tile(t, carry):
            where = lanes(t)
            start = stacked_flat(weight, where) * jnp.exp(-decb[:, :, where] * sublane())

            def sink(rows, value):
                taps[rows, where] = value

            spread_poles(start, pow8[:, :, where], False, sink)
            return carry

        lax.fori_loop(0, tiles, tile, 0)

    def spectra(matrix, source, dst, used):
        def chunk(q, carry):
            where = lanes(q, WIDE)
            high, low = split(source[:, where])
            table = matrix[:, :used]
            dst[:, where] = dot(table, high) + dot(table, low)
            return carry

        lax.fori_loop(0, chunks, chunk, 0)

    def filtered(matrix, back, window, spectrum, adjoint):
        half = matrix.shape[0] // 2
        image = dot(matrix[...], window)
        re, im = image[:half], image[half:]
        hre, him = spectrum[:half], spectrum[half:]
        if adjoint:
            out_re = re * hre + im * him
            out_im = im * hre - re * him
        else:
            out_re = re * hre - im * him
            out_im = re * him + im * hre
        product = jnp.concatenate([out_re.astype(BF16), out_im.astype(BF16)], axis=0)
        return dot(back, product)

    def local_part(src, adjoint):
        def chunk(q, carry):
            where = lanes(q, WIDE)
            local[:, where] = filtered(w2, v2[...], src[:, where], h2[:, where], adjoint)
            return carry

        lax.fori_loop(0, chunks, chunk, 0)

    def scan_one(st, r1, line):
        sent = []
        for d in range(1, YN):
            other = (y + d) % YN
            sent.append(
                pltpu.make_async_remote_copy(
                    src_ref=st.at[other],
                    dst_ref=r1.at[y],
                    send_sem=sc1_send.at[line, d],
                    recv_sem=sc1_recv.at[line, d],
                    device_id={"context": z * YN + other},
                    device_id_type=MESH,
                )
            )
        for copy in sent:
            copy.start()
        r1[y] = st[y]
        return sent

    def finish(sent):
        for copy in sent:
            copy.wait_send()
        for copy in sent:
            copy.wait_recv()

    def rate_here():
        return dect[:, lanes(y, WIDE)]

    def scan_two(sent, r1, tz, r2, line, reverse):
        finish(sent)
        step = jnp.exp(-float(ROWS) * rate_here())
        order = range(YN - 1, -1, -1) if reverse else range(YN)
        total = jnp.zeros((POLES, WIDE), F32)
        for index in order:
            total = total * step + r1[index]
        tz[...] = total
        moved = []
        for d in range(1, zn):
            target = z - d if reverse else z + d
            source = z + d if reverse else z - d
            copy = pltpu.make_async_remote_copy(
                src_ref=tz,
                dst_ref=r2.at[z],
                send_sem=sc2_send.at[line, d],
                recv_sem=sc2_recv.at[line, d],
                device_id={"context": ((target + zn) % zn) * YN + y},
                device_id_type=MESH,
            )
            sends = (target >= 0) if reverse else (target < zn)
            gets = (source < zn) if reverse else (source >= 0)

            @pl.when(sends)
            def _(copy=copy):
                copy.start()

            moved.append((copy, sends, gets))
        return moved

    def scan_three(moved, r1, r2, o3, r3, line, reverse):
        for copy, sends, gets in moved:

            @pl.when(sends)
            def _(copy=copy):
                copy.wait_send()

            @pl.when(gets)
            def _(copy=copy):
                copy.wait_recv()

        rate = rate_here()
        step = jnp.exp(-float(ROWS) * rate)
        group = jnp.exp(-float(ROWS * YN) * rate)
        state = jnp.zeros((POLES, WIDE), F32)
        for d in range(zn - 1, 0, -1):
            source = (z + d) if reverse else (z - d)
            state = state * group + r2[(source + zn) % zn]
        order = range(YN - 1, -1, -1) if reverse else range(YN)
        for index in order:
            o3[index] = state
            state = state * step + r1[index]
        sent = []
        for d in range(1, YN):
            other = (y + d) % YN
            sent.append(
                pltpu.make_async_remote_copy(
                    src_ref=o3.at[other],
                    dst_ref=r3.at[y],
                    send_sem=sc3_send.at[line, d],
                    recv_sem=sc3_recv.at[line, d],
                    device_id={"context": z * YN + other},
                    device_id_type=MESH,
                )
            )
        for copy in sent:
            copy.start()
        r3[y] = o3[y]
        return sent

    def carried(r3, reverse, sink):
        def quarter(q, carry):
            for side in range(2):
                where = lanes(q * 2 + side)
                inner = slice(side * LANE, (side + 1) * LANE)
                place = (8.0 - sublane()) if reverse else (sublane() + 1.0)
                start = (
                    stacked(r3, q, inner)
                    * stacked_flat(weight, where)
                    * jnp.exp(-decb[:, :, where] * place)
                )
                spread_poles(
                    start, pow8[:, :, where], reverse, lambda rows, value: sink(rows, where, value)
                )
            return carry

        lax.fori_loop(0, chunks, quarter, 0)

    def over_tiles(body):
        def step(t, carry):
            body(lanes(t), t)
            return carry

        lax.fori_loop(0, tiles, step, 0)

    def over_chunks(body):
        def step(q, carry):
            body(lanes(q, WIDE))
            return carry

        lax.fori_loop(0, chunks, step, 0)

    def fold(value):
        return sum(value[:, i * LANE : (i + 1) * LANE] for i in range(value.shape[1] // LANE))

    def twice(column):
        return jnp.concatenate([column] * (WIDE // LANE), axis=1)

    loads[0].wait()
    sums[...] = jnp.zeros_like(sums)

    def square_stream(where, t):
        value = x0[:, where].astype(F32)
        sums[...] += value * value

    over_tiles(square_stream)
    psa[0, me] = row_of(sums[...])

    for load in loads[1:5]:
        load.wait()
    pole_tables()

    def cotangent_gate(where, t):
        e2[:, where] = (post[2, :, where].astype(F32) * cot[:, where].astype(F32)).astype(BF16)

    over_tiles(cotangent_gate)
    states(e2, st_b, True)

    pl.semaphore_wait(barrier, len(partners))
    first_sum = exchange(psa.at[0], 0)
    for copy in first_sum:
        copy.start()
    back_one = scan_one(st_b, r1_b, 0)
    for load in loads[5:]:
        load.wait()
    spectra(w1, mr, h1, HALF)

    total = collect(first_sum, psa.at[0])
    s0 = lax.rsqrt(total * (1.0 / channels) + EPSILON)
    col_s[0] = col_of(s0)

    def gate_stream(where, t, rows):
        value = (
            pre[0, rows, where].astype(F32)
            * x0[rows, where].astype(F32)
            * col_s[0, rows, :]
            * gains[0:1, where]
        )
        a0[t, pl.ds(rows.start + 8, rows.stop - rows.start), :] = value.astype(BF16).astype(F32)

    over_tiles(lambda where, t: gate_stream(where, t, slice(240, 256)))
    short_halo = halo(a0.at[:, pl.ds(256, 8), :], a0.at[:, pl.ds(0, 8), :], 0, following)
    short_halo.start()
    over_tiles(lambda where, t: gate_stream(where, t, slice(0, 240)))

    def short_layer(where, t, first, count):
        conv = se[0:1, where] * a0[t, pl.ds(first + 8, count), :]
        for j in range(1, 7):
            conv += se[j : j + 1, where] * a0[t, pl.ds(first + 8 - j, count), :]
        rows = slice(first, first + count)
        value = (x0[rows, where].astype(F32) + post[0, rows, where].astype(F32) * conv).astype(BF16)
        x1[rows, where] = value
        value = value.astype(F32)
        sums[rows, :] += value * value

    sums[...] = jnp.zeros_like(sums)
    over_tiles(lambda where, t: short_layer(where, t, 16, 240))
    short_halo.wait()

    @pl.when(k == 0)
    def _():
        a0[:, 0:8, :] = jnp.zeros((tiles, 8, LANE), F32)

    over_tiles(lambda where, t: short_layer(where, t, 0, 16))
    psa[1, me] = row_of(sums[...])
    second_sum = exchange(psa.at[1], 1)
    for copy in second_sum:
        copy.start()

    back_two = scan_two(back_one, r1_b, tz_b, r2_b, 0, True)
    filter_head()
    spectra(w2, taps, h2, ROWS)

    total = collect(second_sum, psa.at[1])
    s1 = lax.rsqrt(total * (1.0 / channels) + EPSILON)
    col_s[1] = col_of(s1)

    def gate_medium(where, t, rows):
        value = (
            pre[1, rows, where].astype(F32)
            * x1[rows, where].astype(F32)
            * col_s[1, rows, :]
            * gains[1:2, where]
        )
        a1[pl.ds(rows.start + HALF, HALF), where] = value.astype(BF16)

    over_tiles(lambda where, t: gate_medium(where, t, slice(HALF, ROWS)))
    medium_halo = halo(a1.at[pl.ds(ROWS, HALF), :], a1.at[pl.ds(0, HALF), :], 1, following)
    medium_halo.start()
    over_tiles(lambda where, t: gate_medium(where, t, slice(0, HALF)))
    back_three = scan_three(back_two, r1_b, r2_b, o3_b, r3_b, 0, True)

    def medium_layer(where, rows):
        window = a1[pl.ds(rows.start, ROWS), where]
        conv = filtered(w1, v1[HALF:, :], window, h1[:, where], False)
        value = x1[rows, where].astype(F32) + post[1, rows, where].astype(F32) * conv
        x2[rows, where] = value.astype(BF16)

    over_chunks(lambda where: medium_layer(where, slice(HALF, ROWS)))
    local_part(e2, True)
    finish(back_three)

    def back_long(rows, where, value):
        spread = (local[rows, where] + value).astype(BF16).astype(F32)
        u2[rows, where] = spread * pre[2, rows, where].astype(F32) * gains[2:3, where]

    carried(r3_b, True, back_long)
    medium_halo.wait()

    @pl.when(k == 0)
    def _():
        a1[0:HALF, :] = jnp.zeros((HALF, width), BF16)

    over_chunks(lambda where: medium_layer(where, slice(0, HALF)))
    sums[...] = jnp.zeros_like(sums)
    sums2[...] = jnp.zeros_like(sums2)

    def both_sums(where, t):
        value = x2[:, where].astype(F32)
        sums[...] += value * value
        sums2[...] += value * u2[:, where]

    over_tiles(both_sums)
    psb[me] = jnp.concatenate([row_of(sums[...]), row_of(sums2[...])], axis=0)
    third_sum = exchange(psb, 2)
    for copy in third_sum:
        copy.start()
    total = collect(third_sum, psb)
    s2 = lax.rsqrt(total[0:1] * (1.0 / channels) + EPSILON)
    col_s[2] = col_of(s2)
    col_k[...] = col_of(s2 * s2 * s2 * total[1:2] * (1.0 / channels))

    def back_two_rows(where, t, rows):
        value = (
            cot[rows, where].astype(F32)
            + u2[rows, where] * col_s[2, rows, :]
            - x2[rows, where].astype(F32) * col_k[rows, :]
        ).astype(BF16)
        g2[rows, where] = value
        e1[rows, where] = (post[1, rows, where].astype(F32) * value.astype(F32)).astype(BF16)

    over_tiles(lambda where, t: back_two_rows(where, t, slice(0, HALF)))
    medium_back = halo(e1.at[pl.ds(0, HALF), :], e1.at[pl.ds(ROWS, HALF), :], 2, preceding)
    medium_back.start()
    over_tiles(lambda where, t: back_two_rows(where, t, slice(HALF, ROWS)))

    def gate_long(where, t):
        value = (
            pre[2, :, where].astype(F32)
            * x2[:, where].astype(F32)
            * col_s[2]
            * gains[2:3, where]
        )
        a2[:, where] = value.astype(BF16)

    over_tiles(gate_long)
    states(a2, st_f, False)
    fore_one = scan_one(st_f, r1_f, 1)

    sums[...] = jnp.zeros_like(sums)

    def medium_adjoint(where, rows):
        window = e1[pl.ds(rows.start, ROWS), where]
        spread = filtered(w1, v1[:HALF, :], window, h1[:, where], True)
        value = spread * pre[1, rows, where].astype(F32) * gains[1:2, where]
        u1[rows, where] = value
        sums[rows, :] += fold(value * x1[rows, where].astype(F32))

    over_chunks(lambda where: medium_adjoint(where, slice(0, HALF)))
    fore_two = scan_two(fore_one, r1_f, tz_f, r2_f, 1, False)
    medium_back.wait()

    @pl.when(k == kn - 1)
    def _():
        e1[ROWS : ROWS + HALF, :] = jnp.zeros((HALF, width), BF16)

    over_chunks(lambda where: medium_adjoint(where, slice(HALF, ROWS)))
    psa[2, me] = row_of(sums[...])
    fourth_sum = exchange(psa.at[2], 3)
    for copy in fourth_sum:
        copy.start()
    local_part(a2, False)
    total = collect(fourth_sum, psa.at[2])
    col_k[...] = col_of(s1 * s1 * s1 * total * (1.0 / channels))

    def back_one_rows(where, t, rows):
        value = (
            g2[rows, where].astype(F32)
            + u1[rows, where] * col_s[1, rows, :]
            - x1[rows, where].astype(F32) * col_k[rows, :]
        ).astype(BF16)
        g1[rows, where] = value
        e0[t, rows, :] = (
            (post[0, rows, where].astype(F32) * value.astype(F32)).astype(BF16).astype(F32)
        )

    over_tiles(lambda where, t: back_one_rows(where, t, slice(0, 16)))
    short_back = halo(e0.at[:, pl.ds(0, 8), :], e0.at[:, pl.ds(256, 8), :], 3, preceding)
    short_back.start()
    over_tiles(lambda where, t: back_one_rows(where, t, slice(16, ROWS)))
    sums[...] = jnp.zeros_like(sums)

    def short_adjoint(where, t, first, count):
        spread = se[0:1, where] * e0[t, pl.ds(first, count), :]
        for j in range(1, 7):
            spread += se[j : j + 1, where] * e0[t, pl.ds(first + j, count), :]
        rows = slice(first, first + count)
        value = spread * pre[0, rows, where].astype(F32) * gains[0:1, where]
        u0[rows, where] = value
        sums[rows, :] += value * x0[rows, where].astype(F32)

    over_tiles(lambda where, t: short_adjoint(where, t, 0, 240))
    short_back.wait()

    @pl.when(k == kn - 1)
    def _():
        e0[:, 256:264, :] = jnp.zeros((tiles, 8, LANE), F32)

    over_tiles(lambda where, t: short_adjoint(where, t, 240, 16))
    psa[3, me] = row_of(sums[...])
    fifth_sum = exchange(psa.at[3], 4)
    for copy in fifth_sum:
        copy.start()

    fore_three = scan_three(fore_two, r1_f, r2_f, o3_f, r3_f, 1, False)
    total = collect(fifth_sum, psa.at[3])
    col_k[...] = col_of(s0 * s0 * s0 * total * (1.0 / channels))

    def final_rows(where, t):
        value = (
            g1[:, where].astype(F32)
            + u0[:, where] * col_s[0]
            - x0[:, where].astype(F32) * col_k[...]
        )
        grad[:, where] = value.astype(BF16)

    over_tiles(final_rows)
    store_grad = pltpu.make_async_copy(grad, grad_h, store_sem.at[0])
    store_grad.start()
    finish(fore_three)

    def fore_long(rows, where, value):
        conv = (local[rows, where] + value).astype(BF16).astype(F32)
        result = x2[rows, where].astype(F32) + post[2, rows, where].astype(F32) * conv
        out[rows, where] = result.astype(BF16)

    carried(r3_f, False, fore_long)
    store_out = pltpu.make_async_copy(out, out_h, store_sem.at[1])
    store_out.start()
    store_grad.wait()
    store_out.wait()


def per_device(zn, tn, *args):
    stream, pre, post, gains, se, mr, res, dec, cot = args
    width = stream.shape[1]
    channels = width * tn
    tiles = width // LANE
    tables = (
        jnp.asarray(dft_matrix(WIDE, WIDE), BF16),
        jnp.asarray(dft_matrix(WIDE, WIDE).T * (2.0 / WIDE), BF16),
        jnp.asarray(dft_matrix(2 * ROWS, ROWS), BF16),
        jnp.asarray(dft_matrix(2 * ROWS, ROWS).T * (1.0 / ROWS), BF16),
    )
    operands = (stream, pre, post, gains, se, mr, res, dec, cot) + tables
    vmem = pltpu.VMEM
    whole = (ROWS, width)
    scan = (YN, POLES, WIDE)
    scratch = [vmem(o.shape, o.dtype) for o in operands]
    scratch += [
        vmem(whole, BF16),
        vmem(whole, BF16),
        vmem((tiles, ROWS + 8, LANE), F32),
        vmem((tiles, ROWS + 8, LANE), F32),
        vmem((ROWS + HALF, width), BF16),
        vmem((ROWS + HALF, width), BF16),
        vmem(whole, BF16),
        vmem(whole, BF16),
        vmem(whole, F32),
        vmem(whole, F32),
        vmem(whole, F32),
        vmem(whole, BF16),
        vmem(whole, BF16),
        vmem(whole, F32),
        vmem(whole, BF16),
        vmem(whole, BF16),
        vmem((POLES, width), F32),
        vmem((POLES, width), F32),
        vmem((POLES, 8, width), F32),
        vmem((POLES, 8, width), F32),
        vmem(whole, F32),
        vmem((WIDE, width), F32),
        vmem((2 * ROWS, width), F32),
        vmem((ROWS, LANE), F32),
        vmem((ROWS, LANE), F32),
        vmem((3, ROWS, LANE), F32),
        vmem((ROWS, LANE), F32),
        vmem((4, tn, 1, ROWS), F32),
        vmem((tn, 2, ROWS), F32),
        vmem(scan, F32), vmem(scan, F32),
        vmem(scan, F32), vmem(scan, F32),
        vmem(scan[1:], F32), vmem(scan[1:], F32),
        vmem((zn, POLES, WIDE), F32), vmem((zn, POLES, WIDE), F32),
        vmem(scan, F32), vmem(scan, F32),
        vmem(scan, F32), vmem(scan, F32),
    ]
    sem = pltpu.SemaphoreType.DMA
    scratch += [
        sem((17,)), sem((2,)), sem((5, tn)), sem((5, tn)), sem((4,)), sem((4,)),
        sem((2, YN)), sem((2, YN)), sem((2, zn)), sem((2, zn)), sem((2, YN)), sem((2, YN)),
    ]
    any_spec = pl.BlockSpec(memory_space=pl.ANY)
    return pl.pallas_call(
        functools.partial(kernel, zn, tn, channels),
        out_shape=(jax.ShapeDtypeStruct(whole, BF16), jax.ShapeDtypeStruct(whole, BF16)),
        in_specs=[any_spec] * len(operands),
        out_specs=(any_spec, any_spec),
        scratch_shapes=scratch,
        compiler_params=pltpu.CompilerParams(
            collective_id=0, has_side_effects=True, vmem_limit_bytes=40 * 2**20
        ),
        cost_estimate=pl.CostEstimate(
            flops=4_000_000_000, bytes_accessed=7_000_000, transcendentals=500_000
        ),
        name="hyena_group",
    )(*operands)


def solution(mesh):
    zn = mesh.shape["context"] // YN
    tn = mesh.shape["tensor"]
    placed = (
        P("context", "tensor"),
        P(None, "context", "tensor"),
        P(None, "context", "tensor"),
        P(None, "tensor"),
        P(None, "tensor"),
        P(None, "tensor"),
        P("tensor", None),
        P("tensor", None),
        P("context", "tensor"),
    )
    return jax.shard_map(
        functools.partial(per_device, zn, tn),
        mesh=mesh,
        in_specs=placed,
        out_specs=(P("context", "tensor"), P("context", "tensor")),
        check_vma=False,
    )
```

time: 367 us -> 84 us (0.23)
  the two profiles are of different devices: /device:TPU:25 before, /device:TPU:1 now
where the time goes in v1:
time: 84 us; the launch traced here: 83.4 us
  Pallas kernels  68 us (81%)
  local copies, waits for them, and re-layouts  14.8 us (18%)
    pallas_call x1, Pallas kernels, per_device(): pl.pallas_call(functools.partial(kernel, zn, tn, channels), out_shape=(ja...  68 us
    unnamed x26, local copies, waits for them, and re-layouts  14.8 us

profile of v1, /device:TPU:1, one launch (start us, length us, event | category | flops | bytes accessed | tf_op | source)
XLA Modules:
  0.0 83.4 jit_solution(14274064459847301408)
XLA Ops:
  0.6 1.0 %copy.15.res_h = f32[1024,16]{1,0:T(8,128)S(1)} copy(f32[1024,16]{0,1:T(8,128)} %param.19) | data formatting | bytes 131072 | tf_op args[6]
  1.7 1.0 %copy.16.dec_h = f32[1024,16]{1,0:T(8,128)S(1)} copy(f32[1024,16]{0,1:T(8,128)} %param.20) | data formatting | bytes 131072 | tf_op args[7]
  2.7 0.0 copy-start
  2.7 1.4 %copy-done = bf16[3,256,1024]{2,1,0:T(8,128)(2,1)S(1)} copy-done((bf16[3,256,1024]{2,1,0:T(8,128)(2,1)S(1)}, bf16[3,256,1024]{2,1,0:T(8,128)(2,1)}, u32[]{:S(2)}) %copy-start) | copy-done | bytes 1572888
  4.1 0.0 copy-start.1
  4.1 1.4 %copy-done.1 = bf16[3,256,1024]{2,1,0:T(8,128)(2,1)S(1)} copy-done((bf16[3,256,1024]{2,1,0:T(8,128)(2,1)S(1)}, bf16[3,256,1024]{2,1,0:T(8,128)(2,1)}, u32[]{:S(2)}) %copy-start.1) | copy-done | bytes 1572888
  5.5 0.0 copy-start.2
  5.5 1.0 %copy-done.2 = bf16[256,1024]{1,0:T(8,128)(2,1)S(1)} copy-done((bf16[256,1024]{1,0:T(8,128)(2,1)S(1)}, bf16[256,1024]{1,0:T(8,128)(2,1)}, u32[]{:S(2)}) %copy-start.2) | copy-done | bytes 524312
  6.6 0.0 copy-start.3
  6.6 1.0 %copy-done.3 = f32[128,1024]{1,0:T(8,128)S(1)} copy-done((f32[128,1024]{1,0:T(8,128)S(1)}, f32[128,1024]{1,0:T(8,128)}, u32[]{:S(2)}) %copy-start.3) | copy-done | bytes 524312
  7.6 0.0 copy-start.4
  7.6 1.0 %copy-done.4 = bf16[256,1024]{1,0:T(8,128)(2,1)S(1)} copy-done((bf16[256,1024]{1,0:T(8,128)(2,1)S(1)}, bf16[256,1024]{1,0:T(8,128)(2,1)}, u32[]{:S(2)}) %copy-start.4) | copy-done | bytes 524312
  8.7 0.0 copy-start.5
  8.7 0.8 copy-done.5
  9.4 0.0 copy-start.6
  9.4 0.7 copy-done.6
  10.1 0.0 copy-start.7
  10.1 0.9 %copy-done.7 = bf16[256,512]{1,0:T(8,128)(2,1)S(1)} copy-done((bf16[256,512]{1,0:T(8,128)(2,1)S(1)}, bf16[256,512]{1,0:T(8,128)(2,1)}, u32[]{:S(2)}) %copy-start.7) | copy-done | bytes 262168
  11.1 0.9 %copy-done.8 = bf16[512,256]{1,0:T(8,128)(2,1)S(1)} copy-done((bf16[512,256]{1,0:T(8,128)(2,1)S(1)}, bf16[512,256]{1,0:T(8,128)(2,1)}, u32[]{:S(2)}) %copy-start.8) | copy-done | bytes 262168
  12.0 0.9 %copy-done.9 = bf16[256,256]{1,0:T(8,128)(2,1)S(1)} copy-done((bf16[256,256]{1,0:T(8,128)(2,1)S(1)}, bf16[256,256]{1,0:T(8,128)(2,1)}, u32[]{:S(2)}) %copy-start.9) | copy-done | bytes 131096
  12.9 0.9 %copy-done.10 = bf16[256,256]{1,0:T(8,128)(2,1)S(1)} copy-done((bf16[256,256]{1,0:T(8,128)(2,1)S(1)}, bf16[256,256]{1,0:T(8,128)(2,1)}, u32[]{:S(2)}) %copy-start.10) | copy-done | bytes 131096
  13.9 68.0 %hyena_group.1 = (bf16[256,1024]{1,0:T(8,128)(2,1)S(1)}, bf16[256,1024]{1,0:T(8,128)(2,1)S(1)}) custom-call(bf16[256,1024]{1,0:T(8,128)(2,1)S(1)} %copy-done.2, bf16[3,256,1024]{2,1,0:T(8,128)(2,1)S(1)} %copy-done, bf16[3,256,1024]{2,1,0:T(8,128)(2,1)S(1)} %copy-done.1, f32[3,1024]{1,0:T(4,128)S(1)} %copy-done.6, f32[7,1024]{1,0:T(8,128)S(1)} %copy-done.5, ...), custom_call_target="tpu_custom_call" | custom-call | flops 4000000000 | bytes 7000000 | tf_op jit(solution)/shard_map/hyena_group/pallas_call | solution.py:691
  81.8 0.8 copy.19
  82.6 0.8 copy.20
  (3 shorter events, 0.0 us)
Async XLA Ops:
  2.7 1.4 %copy-start = (bf16[3,256,1024]{2,1,0:T(8,128)(2,1)S(1)}, bf16[3,256,1024]{2,1,0:T(8,128)(2,1)}, u32[]{:S(2)}) copy-start(bf16[3,256,1024]{2,1,0:T(8,128)(2,1)} %pre_h.1) | copy-start | bytes 4718596
  4.1 1.4 %copy-start.1 = (bf16[3,256,1024]{2,1,0:T(8,128)(2,1)S(1)}, bf16[3,256,1024]{2,1,0:T(8,128)(2,1)}, u32[]{:S(2)}) copy-start(bf16[3,256,1024]{2,1,0:T(8,128)(2,1)} %post_h.1) | copy-start | bytes 4718596
  5.5 1.0 %copy-start.2 = (bf16[256,1024]{1,0:T(8,128)(2,1)S(1)}, bf16[256,1024]{1,0:T(8,128)(2,1)}, u32[]{:S(2)}) copy-start(bf16[256,1024]{1,0:T(8,128)(2,1)} %stream_h.1) | copy-start | bytes 1572868
  6.6 1.0 %copy-start.3 = (f32[128,1024]{1,0:T(8,128)S(1)}, f32[128,1024]{1,0:T(8,128)}, u32[]{:S(2)}) copy-start(f32[128,1024]{1,0:T(8,128)} %mr_h.1) | copy-start | bytes 1572868
  7.6 1.0 %copy-start.4 = (bf16[256,1024]{1,0:T(8,128)(2,1)S(1)}, bf16[256,1024]{1,0:T(8,128)(2,1)}, u32[]{:S(2)}) copy-start(bf16[256,1024]{1,0:T(8,128)(2,1)} %cot_h.1) | copy-start | bytes 1572868
  8.7 0.8 copy-start.5
  9.4 0.7 copy-start.6
  10.1 0.9 %copy-start.7 = (bf16[256,512]{1,0:T(8,128)(2,1)S(1)}, bf16[256,512]{1,0:T(8,128)(2,1)}, u32[]{:S(2)}) copy-start(bf16[256,512]{1,0:T(8,128)(2,1)} %constant.11.clone.v2_h) | copy-start | bytes 786436
  11.1 0.9 %copy-start.8 = (bf16[512,256]{1,0:T(8,128)(2,1)S(1)}, bf16[512,256]{1,0:T(8,128)(2,1)}, u32[]{:S(2)}) copy-start(bf16[512,256]{1,0:T(8,128)(2,1)} %constant.10.clone.w2_h) | copy-start | bytes 786436
  12.0 0.9 %copy-start.9 = (bf16[256,256]{1,0:T(8,128)(2,1)S(1)}, bf16[256,256]{1,0:T(8,128)(2,1)}, u32[]{:S(2)}) copy-start(bf16[256,256]{1,0:T(8,128)(2,1)} %constant.9.clone.v1_h) | copy-start | bytes 393220
  12.9 0.9 %copy-start.10 = (bf16[256,256]{1,0:T(8,128)(2,1)S(1)}, bf16[256,256]{1,0:T(8,128)(2,1)}, u32[]{:S(2)}) copy-start(bf16[256,256]{1,0:T(8,128)(2,1)} %constant.8.clone.w1_h) | copy-start | bytes 393220

commit v2 on v1

--- a/solution.py
+++ b/solution.py
@@ -46,10 +46,10 @@
     channels,
     stream_h, pre_h, post_h, gains_h, se_h, mr_h, res_h, dec_h, cot_h, w1_h, v1_h, w2_h, v2_h,
     out_h, grad_h,
-    x0, pre, post, gains, se, mr, res, dec, cot, w1, v1, w2, v2,
+    x0, pre, post, gains, se, mr, res, dect, cot, w1, v1, w2, v2,
     x1, x2, a0, e0, a1, e1, e2, a2, u0, u1, u2, g1, g2, local, out, grad,
-    dect, weight, decb, pow8, taps, h1, h2,
-    sums, sums2, col_s, col_k, psa, psb,
+    weight, decb, pow8, taps, h1, h2,
+    sums, sums2, col_s, col_k, ps0, psh, ps2,
     st_b, st_f, r1_b, r1_f, tz_b, tz_f, r2_b, r2_f, o3_b, o3_f, r3_b, r3_f,
     load_sem, store_sem, ps_send, ps_recv, halo_send, halo_recv,
     sc1_send, sc1_recv, sc2_send, sc2_recv, sc3_send, sc3_recv,
@@ -66,7 +66,7 @@
     preceding = (k + kn - 1) % kn
 
     plan = [
-        (stream_h, x0), (dec_h, dec), (res_h, res), (cot_h, cot), (post_h.at[2], post.at[2]),
+        (stream_h, x0), (dec_h, dect), (res_h, res), (cot_h, cot), (post_h.at[2], post.at[2]),
         (w1_h, w1), (mr_h, mr), (gains_h, gains), (se_h, se), (w2_h, w2), (v2_h, v2), (v1_h, v1),
         (pre_h.at[0], pre.at[0]), (post_h.at[0], post.at[0]), (pre_h.at[1], pre.at[1]),
         (post_h.at[1], post.at[1]), (pre_h.at[2], pre.at[2]),
@@ -90,7 +90,9 @@
         return jnp.sum(total.T, axis=0, keepdims=True)
 
     def col_of(row):
-        return jnp.broadcast_to(row, (LANE, ROWS)).T
+        return jnp.broadcast_to(row, (LANE, row.shape[1])).T
+
+    leaving = []
 
     def exchange(slots, phase):
         sent = []
@@ -105,11 +107,12 @@
                     device_id_type=MESH,
                 )
             )
+        for copy in sent:
+            copy.start()
+        leaving.extend(sent)
         return sent
 
     def collect(sent, slots):
-        for copy in sent:
-            copy.wait_send()
         for copy in sent:
             copy.wait_recv()
         total = slots[0]
@@ -118,7 +121,7 @@
         return total
 
     def halo(src, dst, index, target):
-        return pltpu.make_async_remote_copy(
+        copy = pltpu.make_async_remote_copy(
             src_ref=src,
             dst_ref=dst,
             send_sem=halo_send.at[index],
@@ -126,18 +129,17 @@
             device_id={"context": target},
             device_id_type=MESH,
         )
+        copy.start()
+        leaving.append(copy)
+        return copy
 
     def pole_tables():
-        for part in range(tiles):
-            here = slice(part * LANE, (part + 1) * LANE)
-            dect[:, here] = dec[here, :].T
-            weight[:, here] = res[here, :].T
         rate = dect[...]
         square = rate * rate
         series = rate * (
             1.0 + square * (1.0 / 6.0) * (1.0 + square * (1.0 / 20.0) * (1.0 + square * (1.0 / 42.0)))
         )
-        weight[...] = weight[...] * jnp.sqrt(2.0 * jnp.exp(-rate) * series)
+        weight[...] = res[...] * jnp.sqrt(2.0 * jnp.exp(-rate) * series)
         for r in range(POLES):
             wide = jnp.broadcast_to(dect[r : r + 1, :], (8, width))
             decb[r] = wide
@@ -161,7 +163,7 @@
                     total = total * base + first[None]
                     return total * base + second[None]
 
-                total = lax.fori_loop(0, ROWS // 16, step, total)
+                total = lax.fori_loop(0, ROWS // 16, step, total, unroll=True)
                 place = sublane() if reverse else 7.0 - sublane()
                 total = total * jnp.exp(-decb[:, :, where] * place)
                 dst[q, :, side * LANE : (side + 1) * LANE] = jnp.sum(total, axis=1)
@@ -181,7 +183,7 @@
             sink(rows, jnp.concatenate(pair, axis=0))
             return state
 
-        lax.fori_loop(0, ROWS // 16, step, start)
+        lax.fori_loop(0, ROWS // 16, step, start, unroll=True)
 
     def stacked(ref, index, where):
         return jnp.stack(
@@ -211,10 +213,12 @@
             where = lanes(q, WIDE)
             high, low = split(source[:, where])
             table = matrix[:, :used]
-            dst[:, where] = dot(table, high) + dot(table, low)
+            dst[:, where] = dot(
+                jnp.concatenate([table, table], axis=1), jnp.concatenate([high, low], axis=0)
+            )
             return carry
 
-        lax.fori_loop(0, chunks, chunk, 0)
+        lax.fori_loop(0, chunks, chunk, 0, unroll=True)
 
     def filtered(matrix, back, window, spectrum, adjoint):
         half = matrix.shape[0] // 2
@@ -236,7 +240,7 @@
             local[:, where] = filtered(w2, v2[...], src[:, where], h2[:, where], adjoint)
             return carry
 
-        lax.fori_loop(0, chunks, chunk, 0)
+        lax.fori_loop(0, chunks, chunk, 0, unroll=True)
 
     def scan_one(st, r1, line):
         sent = []
@@ -254,12 +258,11 @@
             )
         for copy in sent:
             copy.start()
+        leaving.extend(sent)
         r1[y] = st[y]
         return sent
 
     def finish(sent):
-        for copy in sent:
-            copy.wait_send()
         for copy in sent:
             copy.wait_recv()
 
@@ -298,10 +301,6 @@
 
     def scan_three(moved, r1, r2, o3, r3, line, reverse):
         for copy, sends, gets in moved:
-
-            @pl.when(sends)
-            def _(copy=copy):
-                copy.wait_send()
 
             @pl.when(gets)
             def _(copy=copy):
@@ -333,6 +332,7 @@
             )
         for copy in sent:
             copy.start()
+        leaving.extend(sent)
         r3[y] = o3[y]
         return sent
 
@@ -366,7 +366,7 @@
             body(lanes(q, WIDE))
             return carry
 
-        lax.fori_loop(0, chunks, step, 0)
+        lax.fori_loop(0, chunks, step, 0, unroll=True)
 
     def fold(value):
         return sum(value[:, i * LANE : (i + 1) * LANE] for i in range(value.shape[1] // LANE))
@@ -374,15 +374,32 @@
     def twice(column):
         return jnp.concatenate([column] * (WIDE // LANE), axis=1)
 
+    low = slice(0, HALF)
+    high = slice(HALF, ROWS)
+
+    def inverse(total):
+        return lax.rsqrt(total * (1.0 / channels) + EPSILON)
+
+    def clear(rows):
+        sums[rows, :] = jnp.zeros((HALF, LANE), F32)
+        sums2[rows, :] = jnp.zeros((HALF, LANE), F32)
+
+    def part(q):
+        return slice(q * WIDE, (q + 1) * WIDE)
+
     loads[0].wait()
-    sums[...] = jnp.zeros_like(sums)
+    clear(low)
+    clear(high)
 
     def square_stream(where, t):
         value = x0[:, where].astype(F32)
         sums[...] += value * value
 
     over_tiles(square_stream)
-    psa[0, me] = row_of(sums[...])
+    ps0[0, me] = row_of(sums[...])
+
+    pl.semaphore_wait(barrier, len(partners))
+    sent_s0 = exchange(ps0.at[0], 0)
 
     for load in loads[1:5]:
         load.wait()
@@ -393,33 +410,23 @@
 
     over_tiles(cotangent_gate)
     states(e2, st_b, True)
-
-    pl.semaphore_wait(barrier, len(partners))
-    first_sum = exchange(psa.at[0], 0)
-    for copy in first_sum:
-        copy.start()
     back_one = scan_one(st_b, r1_b, 0)
     for load in loads[5:]:
         load.wait()
     spectra(w1, mr, h1, HALF)
 
-    total = collect(first_sum, psa.at[0])
-    s0 = lax.rsqrt(total * (1.0 / channels) + EPSILON)
+    s0 = inverse(collect(sent_s0, ps0.at[0]))
     col_s[0] = col_of(s0)
 
-    def gate_stream(where, t, rows):
+    def gate_stream(where, t, first, count):
+        rows = slice(first, first + count)
         value = (
             pre[0, rows, where].astype(F32)
             * x0[rows, where].astype(F32)
             * col_s[0, rows, :]
             * gains[0:1, where]
         )
-        a0[t, pl.ds(rows.start + 8, rows.stop - rows.start), :] = value.astype(BF16).astype(F32)
-
-    over_tiles(lambda where, t: gate_stream(where, t, slice(240, 256)))
-    short_halo = halo(a0.at[:, pl.ds(256, 8), :], a0.at[:, pl.ds(0, 8), :], 0, following)
-    short_halo.start()
-    over_tiles(lambda where, t: gate_stream(where, t, slice(0, 240)))
+        a0[t, pl.ds(first + 8, count), :] = value.astype(BF16).astype(F32)
 
     def short_layer(where, t, first, count):
         conv = se[0:1, where] * a0[t, pl.ds(first + 8, count), :]
@@ -431,51 +438,66 @@
         value = value.astype(F32)
         sums[rows, :] += value * value
 
-    sums[...] = jnp.zeros_like(sums)
-    over_tiles(lambda where, t: short_layer(where, t, 16, 240))
-    short_halo.wait()
+    over_tiles(lambda where, t: gate_stream(where, t, 240, 16))
+    short_halo = halo(a0.at[:, pl.ds(256, 8), :], a0.at[:, pl.ds(0, 8), :], 0, following)
+    over_tiles(lambda where, t: gate_stream(where, t, 112, 128))
+    clear(low)
+    clear(high)
+    over_tiles(lambda where, t: short_layer(where, t, 128, 128))
+    psh[0, me] = row_of(sums[high, :])
+    sent_s1_high = exchange(psh.at[0], 1)
+
+    back_two = scan_two(back_one, r1_b, tz_b, r2_b, 0, True)
+    over_tiles(lambda where, t: gate_stream(where, t, 0, 112))
+    over_tiles(lambda where, t: short_layer(where, t, 16, 112))
+    filter_head()
+    short_halo.wait_recv()
 
     @pl.when(k == 0)
     def _():
         a0[:, 0:8, :] = jnp.zeros((tiles, 8, LANE), F32)
 
     over_tiles(lambda where, t: short_layer(where, t, 0, 16))
-    psa[1, me] = row_of(sums[...])
-    second_sum = exchange(psa.at[1], 1)
-    for copy in second_sum:
-        copy.start()
-
-    back_two = scan_two(back_one, r1_b, tz_b, r2_b, 0, True)
-    filter_head()
+    psh[1, me] = row_of(sums[low, :])
+    sent_s1_low = exchange(psh.at[1], 2)
     spectra(w2, taps, h2, ROWS)
 
-    total = collect(second_sum, psa.at[1])
-    s1 = lax.rsqrt(total * (1.0 / channels) + EPSILON)
-    col_s[1] = col_of(s1)
-
-    def gate_medium(where, t, rows):
+    def gate_medium(where, rows, column):
         value = (
             pre[1, rows, where].astype(F32)
             * x1[rows, where].astype(F32)
-            * col_s[1, rows, :]
+            * twice(column)
             * gains[1:2, where]
         )
         a1[pl.ds(rows.start + HALF, HALF), where] = value.astype(BF16)
-
-    over_tiles(lambda where, t: gate_medium(where, t, slice(HALF, ROWS)))
-    medium_halo = halo(a1.at[pl.ds(ROWS, HALF), :], a1.at[pl.ds(0, HALF), :], 1, following)
-    medium_halo.start()
-    over_tiles(lambda where, t: gate_medium(where, t, slice(0, HALF)))
-    back_three = scan_three(back_two, r1_b, r2_b, o3_b, r3_b, 0, True)
 
     def medium_layer(where, rows):
         window = a1[pl.ds(rows.start, ROWS), where]
         conv = filtered(w1, v1[HALF:, :], window, h1[:, where], False)
-        value = x1[rows, where].astype(F32) + post[1, rows, where].astype(F32) * conv
-        x2[rows, where] = value.astype(BF16)
-
-    over_chunks(lambda where: medium_layer(where, slice(HALF, ROWS)))
+        value = (
+            x1[rows, where].astype(F32) + post[1, rows, where].astype(F32) * conv
+        ).astype(BF16)
+        x2[rows, where] = value
+        value = value.astype(F32)
+        sums[rows, :] += fold(value * value)
+
+    s1_high = inverse(collect(sent_s1_high, psh.at[0]))
+    col_s[1, high] = col_of(s1_high)
+    medium_halo = []
+    for q in range(chunks):
+        gate_medium(part(q), high, col_s[1, high])
+        medium_halo.append(
+            halo(a1.at[pl.ds(ROWS, HALF), part(q)], a1.at[pl.ds(0, HALF), part(q)], 2 + q, following)
+        )
+
     local_part(e2, True)
+    back_three = scan_three(back_two, r1_b, r2_b, o3_b, r3_b, 0, True)
+    s1_low = inverse(collect(sent_s1_low, psh.at[1]))
+    col_s[1, low] = col_of(s1_low)
+    over_chunks(lambda where: gate_medium(where, low, col_s[1, low]))
+    clear(low)
+    clear(high)
+    over_chunks(lambda where: medium_layer(where, high))
     finish(back_three)
 
     def back_long(rows, where, value):
@@ -483,44 +505,50 @@
         u2[rows, where] = spread * pre[2, rows, where].astype(F32) * gains[2:3, where]
 
     carried(r3_b, True, back_long)
-    medium_halo.wait()
-
-    @pl.when(k == 0)
-    def _():
-        a1[0:HALF, :] = jnp.zeros((HALF, width), BF16)
-
-    over_chunks(lambda where: medium_layer(where, slice(0, HALF)))
-    sums[...] = jnp.zeros_like(sums)
-    sums2[...] = jnp.zeros_like(sums2)
-
-    def both_sums(where, t):
-        value = x2[:, where].astype(F32)
-        sums[...] += value * value
-        sums2[...] += value * u2[:, where]
-
-    over_tiles(both_sums)
-    psb[me] = jnp.concatenate([row_of(sums[...]), row_of(sums2[...])], axis=0)
-    third_sum = exchange(psb, 2)
-    for copy in third_sum:
-        copy.start()
-    total = collect(third_sum, psb)
-    s2 = lax.rsqrt(total[0:1] * (1.0 / channels) + EPSILON)
-    col_s[2] = col_of(s2)
-    col_k[...] = col_of(s2 * s2 * s2 * total[1:2] * (1.0 / channels))
-
-    def back_two_rows(where, t, rows):
+
+    def inner_sums(where, rows):
+        sums2[rows, :] += x2[rows, where].astype(F32) * u2[rows, where]
+
+    over_tiles(lambda where, t: inner_sums(where, high))
+    ps2[0, me] = jnp.concatenate([row_of(sums[high, :]), row_of(sums2[high, :])], axis=0)
+    sent_s2_high = exchange(ps2.at[0], 3)
+
+    for q in range(chunks):
+        medium_halo[q].wait_recv()
+
+        @pl.when(k == 0)
+        def _(q=q):
+            a1[0:HALF, part(q)] = jnp.zeros((HALF, WIDE), BF16)
+
+        medium_layer(part(q), low)
+        sums2[low, :] += fold(x2[low, part(q)].astype(F32) * u2[low, part(q)])
+    ps2[1, me] = jnp.concatenate([row_of(sums[low, :]), row_of(sums2[low, :])], axis=0)
+    sent_s2_low = exchange(ps2.at[1], 4)
+
+    def second_columns(sent, slots, rows):
+        total = collect(sent, slots)
+        s2 = inverse(total[0:1])
+        col_s[2, rows] = col_of(s2)
+        col_k[rows, :] = col_of(s2 * s2 * s2 * total[1:2] * (1.0 / channels))
+
+    def back_two_rows(where, rows):
         value = (
             cot[rows, where].astype(F32)
-            + u2[rows, where] * col_s[2, rows, :]
-            - x2[rows, where].astype(F32) * col_k[rows, :]
+            + u2[rows, where] * twice(col_s[2, rows])
+            - x2[rows, where].astype(F32) * twice(col_k[rows, :])
         ).astype(BF16)
         g2[rows, where] = value
         e1[rows, where] = (post[1, rows, where].astype(F32) * value.astype(F32)).astype(BF16)
 
-    over_tiles(lambda where, t: back_two_rows(where, t, slice(0, HALF)))
-    medium_back = halo(e1.at[pl.ds(0, HALF), :], e1.at[pl.ds(ROWS, HALF), :], 2, preceding)
-    medium_back.start()
-    over_tiles(lambda where, t: back_two_rows(where, t, slice(HALF, ROWS)))
+    second_columns(sent_s2_low, ps2.at[1], low)
+    medium_back = []
+    for q in range(chunks):
+        back_two_rows(part(q), low)
+        medium_back.append(
+            halo(e1.at[pl.ds(0, HALF), part(q)], e1.at[pl.ds(ROWS, HALF), part(q)], 6 + q, preceding)
+        )
+    second_columns(sent_s2_high, ps2.at[0], high)
+    over_chunks(lambda where: back_two_rows(where, high))
 
     def gate_long(where, t):
         value = (
@@ -535,7 +563,8 @@
     states(a2, st_f, False)
     fore_one = scan_one(st_f, r1_f, 1)
 
-    sums[...] = jnp.zeros_like(sums)
+    clear(low)
+    clear(high)
 
     def medium_adjoint(where, rows):
         window = e1[pl.ds(rows.start, ROWS), where]
@@ -544,22 +573,11 @@
         u1[rows, where] = value
         sums[rows, :] += fold(value * x1[rows, where].astype(F32))
 
-    over_chunks(lambda where: medium_adjoint(where, slice(0, HALF)))
+    over_chunks(lambda where: medium_adjoint(where, low))
+    psh[2, me] = row_of(sums[low, :])
+    sent_m1_low = exchange(psh.at[2], 5)
+    local_part(a2, False)
     fore_two = scan_two(fore_one, r1_f, tz_f, r2_f, 1, False)
-    medium_back.wait()
-
-    @pl.when(k == kn - 1)
-    def _():
-        e1[ROWS : ROWS + HALF, :] = jnp.zeros((HALF, width), BF16)
-
-    over_chunks(lambda where: medium_adjoint(where, slice(HALF, ROWS)))
-    psa[2, me] = row_of(sums[...])
-    fourth_sum = exchange(psa.at[2], 3)
-    for copy in fourth_sum:
-        copy.start()
-    local_part(a2, False)
-    total = collect(fourth_sum, psa.at[2])
-    col_k[...] = col_of(s1 * s1 * s1 * total * (1.0 / channels))
 
     def back_one_rows(where, t, rows):
         value = (
@@ -572,12 +590,6 @@
             (post[0, rows, where].astype(F32) * value.astype(F32)).astype(BF16).astype(F32)
         )
 
-    over_tiles(lambda where, t: back_one_rows(where, t, slice(0, 16)))
-    short_back = halo(e0.at[:, pl.ds(0, 8), :], e0.at[:, pl.ds(256, 8), :], 3, preceding)
-    short_back.start()
-    over_tiles(lambda where, t: back_one_rows(where, t, slice(16, ROWS)))
-    sums[...] = jnp.zeros_like(sums)
-
     def short_adjoint(where, t, first, count):
         spread = se[0:1, where] * e0[t, pl.ds(first, count), :]
         for j in range(1, 7):
@@ -585,23 +597,50 @@
         rows = slice(first, first + count)
         value = spread * pre[0, rows, where].astype(F32) * gains[0:1, where]
         u0[rows, where] = value
-        sums[rows, :] += value * x0[rows, where].astype(F32)
-
-    over_tiles(lambda where, t: short_adjoint(where, t, 0, 240))
-    short_back.wait()
+        sums2[rows, :] += value * x0[rows, where].astype(F32)
+
+    total = collect(sent_m1_low, psh.at[2])
+    col_k[low, :] = col_of(s1_low * s1_low * s1_low * total * (1.0 / channels))
+    over_tiles(lambda where, t: back_one_rows(where, t, low))
+    short_back = halo(e0.at[:, pl.ds(0, 8), :], e0.at[:, pl.ds(256, 8), :], 1, preceding)
+    over_tiles(lambda where, t: short_adjoint(where, t, 0, 112))
+
+    for q in range(chunks):
+        medium_back[q].wait_recv()
+
+        @pl.when(k == kn - 1)
+        def _(q=q):
+            e1[ROWS : ROWS + HALF, part(q)] = jnp.zeros((HALF, WIDE), BF16)
+
+        medium_adjoint(part(q), high)
+    psh[3, me] = row_of(sums[high, :])
+    sent_m1_high = exchange(psh.at[3], 6)
+    fore_three = scan_three(fore_two, r1_f, r2_f, o3_f, r3_f, 1, False)
+    short_back.wait_recv()
 
     @pl.when(k == kn - 1)
     def _():
         e0[:, 256:264, :] = jnp.zeros((tiles, 8, LANE), F32)
 
-    over_tiles(lambda where, t: short_adjoint(where, t, 240, 16))
-    psa[3, me] = row_of(sums[...])
-    fifth_sum = exchange(psa.at[3], 4)
-    for copy in fifth_sum:
-        copy.start()
-
-    fore_three = scan_three(fore_two, r1_f, r2_f, o3_f, r3_f, 1, False)
-    total = collect(fifth_sum, psa.at[3])
+    total = collect(sent_m1_high, psh.at[3])
+    col_k[high, :] = col_of(s1_high * s1_high * s1_high * total * (1.0 / channels))
+    over_tiles(lambda where, t: back_one_rows(where, t, high))
+    over_tiles(lambda where, t: short_adjoint(where, t, 112, 144))
+    ps0[1, me] = row_of(sums2[...])
+    sent_m0 = exchange(ps0.at[1], 7)
+
+    finish(fore_three)
+
+    def fore_long(rows, where, value):
+        conv = (local[rows, where] + value).astype(BF16).astype(F32)
+        result = x2[rows, where].astype(F32) + post[2, rows, where].astype(F32) * conv
+        out[rows, where] = result.astype(BF16)
+
+    carried(r3_f, False, fore_long)
+    store_out = pltpu.make_async_copy(out, out_h, store_sem.at[1])
+    store_out.start()
+
+    total = collect(sent_m0, ps0.at[1])
     col_k[...] = col_of(s0 * s0 * s0 * total * (1.0 / channels))
 
     def final_rows(where, t):
@@ -615,18 +654,16 @@
     over_tiles(final_rows)
     store_grad = pltpu.make_async_copy(grad, grad_h, store_sem.at[0])
     store_grad.start()
-    finish(fore_three)
-
-    def fore_long(rows, where, value):
-        conv = (local[rows, where] + value).astype(BF16).astype(F32)
-        result = x2[rows, where].astype(F32) + post[2, rows, where].astype(F32) * conv
-        out[rows, where] = result.astype(BF16)
-
-    carried(r3_f, False, fore_long)
-    store_out = pltpu.make_async_copy(out, out_h, store_sem.at[1])
-    store_out.start()
+    for copy in leaving:
+        copy.wait_send()
+    for copy, sends, gets in back_two + fore_two:
+
+        @pl.when(sends)
+        def _(copy=copy):
+            copy.wait_send()
+
+    store_out.wait()
     store_grad.wait()
-    store_out.wait()
 
 
 def per_device(zn, tn, *args):
@@ -640,7 +677,7 @@
         jnp.asarray(dft_matrix(2 * ROWS, ROWS), BF16),
         jnp.asarray(dft_matrix(2 * ROWS, ROWS).T * (1.0 / ROWS), BF16),
     )
-    operands = (stream, pre, post, gains, se, mr, res, dec, cot) + tables
+    operands = (stream, pre, post, gains, se, mr, res.T, dec.T, cot) + tables
     vmem = pltpu.VMEM
     whole = (ROWS, width)
     scan = (YN, POLES, WIDE)
@@ -663,7 +700,6 @@
         vmem(whole, BF16),
         vmem(whole, BF16),
         vmem((POLES, width), F32),
-        vmem((POLES, width), F32),
         vmem((POLES, 8, width), F32),
         vmem((POLES, 8, width), F32),
         vmem(whole, F32),
@@ -673,8 +709,9 @@
         vmem((ROWS, LANE), F32),
         vmem((3, ROWS, LANE), F32),
         vmem((ROWS, LANE), F32),
-        vmem((4, tn, 1, ROWS), F32),
-        vmem((tn, 2, ROWS), F32),
+        vmem((2, tn, 1, ROWS), F32),
+        vmem((4, tn, 1, HALF), F32),
+        vmem((2, tn, 2, HALF), F32),
         vmem(scan, F32), vmem(scan, F32),
         vmem(scan, F32), vmem(scan, F32),
         vmem(scan[1:], F32), vmem(scan[1:], F32),
@@ -684,7 +721,7 @@
     ]
     sem = pltpu.SemaphoreType.DMA
     scratch += [
-        sem((17,)), sem((2,)), sem((5, tn)), sem((5, tn)), sem((4,)), sem((4,)),
+        sem((17,)), sem((2,)), sem((8, tn)), sem((8, tn)), sem((10,)), sem((10,)),
         sem((2, YN)), sem((2, YN)), sem((2, zn)), sem((2, zn)), sem((2, YN)), sem((2, YN)),
     ]
     any_spec = pl.BlockSpec(memory_space=pl.ANY)
@@ -695,7 +732,7 @@
         out_specs=(any_spec, any_spec),
         scratch_shapes=scratch,
         compiler_params=pltpu.CompilerParams(
-            collective_id=0, has_side_effects=True, vmem_limit_bytes=40 * 2**20
+            collective_id=0, has_side_effects=True, vmem_limit_bytes=60 * 2**20
         ),
         cost_estimate=pl.CostEstimate(
             flops=4_000_000_000, bytes_accessed=7_000_000, transcendentals=500_000

time: 84 us -> 60.5 us (0.72)
  Pallas kernels: 68 us -> 55.7 us
  local copies, waits for them, and re-layouts: 14.8 us -> 3.74 us
    pallas_call x1, Pallas kernels: 68 us -> 55.7 us  [per_device(): pl.pallas_call(functools.partial(kernel, zn, tn, channels), out_shape=(ja...]
    unnamed x26 -> x2, local copies, waits for them, and re-layouts: 14.8 us -> 3.74 us
where the time goes in v2:
time: 60.5 us; the launch traced here: 60.1 us
  Pallas kernels  55.7 us (92%)
  local copies, waits for them, and re-layouts  3.74 us (6%)
  between operations  0.64 us (1%)
    pallas_call x1, Pallas kernels, per_device(): pl.pallas_call(functools.partial(kernel, zn, tn, channels), out_shape=(ja...  55.7 us
    unnamed x2, local copies, waits for them, and re-layouts  3.74 us

profile of v2, /device:TPU:1, one launch (start us, length us, event | category | flops | bytes accessed | tf_op | source)
XLA Modules:
  0.0 60.1 jit_solution(10643696600008312527)
XLA Ops:
  0.6 55.7 %hyena_group.1 = (bf16[256,1024]{1,0:T(8,128)(2,1)}, bf16[256,1024]{1,0:T(8,128)(2,1)}) custom-call(bf16[256,1024]{1,0:T(8,128)(2,1)} %stream_h.1, bf16[3,256,1024]{2,1,0:T(8,128)(2,1)} %pre_h.1, bf16[3,256,1024]{2,1,0:T(8,128)(2,1)} %post_h.1, f32[3,1024]{1,0:T(4,128)} %gains_h.1, f32[7,1024]{1,0:T(8,128)} %se_h.1, f32[128,1024]{1,0:T(8,128)} %mr_h.1, ...), custom_call_target="tpu_custom_call" | custom-call | flops 4000000000 | bytes 7000000 | tf_op jit(solution)/shard_map/hyena_group/pallas_call | solution.py:728
  56.3 1.9 %copy.17 = bf16[256,1024]{1,0:T(8,128)(2,1)} copy(bf16[256,1024]{1,0:T(8,128)(2,1)} %get-tuple-element.4) | data formatting | bytes 1048576
  58.2 1.9 %copy.18 = bf16[256,1024]{1,0:T(8,128)(2,1)} copy(bf16[256,1024]{1,0:T(8,128)(2,1)} %get-tuple-element.5) | data formatting | bytes 1048576

commit v3 on v2

--- a/solution.py
+++ b/solution.py
@@ -45,11 +45,11 @@
     tn,
     channels,
     stream_h, pre_h, post_h, gains_h, se_h, mr_h, res_h, dec_h, cot_h, w1_h, v1_h, w2_h, v2_h,
-    out_h, grad_h,
+    both_h,
     x0, pre, post, gains, se, mr, res, dect, cot, w1, v1, w2, v2,
     x1, x2, a0, e0, a1, e1, e2, a2, u0, u1, u2, g1, g2, local, out, grad,
     weight, decb, pow8, taps, h1, h2,
-    sums, sums2, col_s, col_k, ps0, psh, ps2,
+    ahead, x1h, s1r, col_h, sums, sums2, col_s, col_k, ps0, psh, ps2,
     st_b, st_f, r1_b, r1_f, tz_b, tz_f, r2_b, r2_f, o3_b, o3_f, r3_b, r3_f,
     load_sem, store_sem, ps_send, ps_recv, halo_send, halo_recv,
     sc1_send, sc1_recv, sc2_send, sc2_recv, sc3_send, sc3_recv,
@@ -398,9 +398,6 @@
     over_tiles(square_stream)
     ps0[0, me] = row_of(sums[...])
 
-    pl.semaphore_wait(barrier, len(partners))
-    sent_s0 = exchange(ps0.at[0], 0)
-
     for load in loads[1:5]:
         load.wait()
     pole_tables()
@@ -410,10 +407,17 @@
 
     over_tiles(cotangent_gate)
     states(e2, st_b, True)
+
+    pl.semaphore_wait(barrier, len(partners))
+    sent_s0 = exchange(ps0.at[0], 0)
+
     back_one = scan_one(st_b, r1_b, 0)
     for load in loads[5:]:
         load.wait()
+    filter_head()
     spectra(w1, mr, h1, HALF)
+    spectra(w2, taps, h2, ROWS)
+    back_two = scan_two(back_one, r1_b, tz_b, r2_b, 0, True)
 
     s0 = inverse(collect(sent_s0, ps0.at[0]))
     col_s[0] = col_of(s0)
@@ -443,14 +447,22 @@
     over_tiles(lambda where, t: gate_stream(where, t, 112, 128))
     clear(low)
     clear(high)
-    over_tiles(lambda where, t: short_layer(where, t, 128, 128))
+    stream_ahead = []
+    for q in range(chunks):
+        for t in range(q * WIDE // LANE, (q + 1) * WIDE // LANE):
+            short_layer(slice(t * LANE, (t + 1) * LANE), t, 128, 128)
+        gated = (
+            pre[1, high, part(q)].astype(F32)
+            * x1[high, part(q)].astype(F32)
+            * gains[1:2, part(q)]
+        )
+        ahead[:, part(q)] = gated.astype(BF16)
+        stream_ahead.append(halo(ahead.at[:, part(q)], x1h.at[:, part(q)], 2 + q, following))
     psh[0, me] = row_of(sums[high, :])
     sent_s1_high = exchange(psh.at[0], 1)
 
-    back_two = scan_two(back_one, r1_b, tz_b, r2_b, 0, True)
     over_tiles(lambda where, t: gate_stream(where, t, 0, 112))
     over_tiles(lambda where, t: short_layer(where, t, 16, 112))
-    filter_head()
     short_halo.wait_recv()
 
     @pl.when(k == 0)
@@ -460,7 +472,7 @@
     over_tiles(lambda where, t: short_layer(where, t, 0, 16))
     psh[1, me] = row_of(sums[low, :])
     sent_s1_low = exchange(psh.at[1], 2)
-    spectra(w2, taps, h2, ROWS)
+    local_part(e2, True)
 
     def gate_medium(where, rows, column):
         value = (
@@ -483,47 +495,42 @@
 
     s1_high = inverse(collect(sent_s1_high, psh.at[0]))
     col_s[1, high] = col_of(s1_high)
-    medium_halo = []
-    for q in range(chunks):
-        gate_medium(part(q), high, col_s[1, high])
-        medium_halo.append(
-            halo(a1.at[pl.ds(ROWS, HALF), part(q)], a1.at[pl.ds(0, HALF), part(q)], 2 + q, following)
-        )
-
-    local_part(e2, True)
+    s1r[0] = s1_high
+    scale_ahead = halo(s1r.at[0], s1r.at[1], 10, following)
+    over_chunks(lambda where: gate_medium(where, high, col_s[1, high]))
     back_three = scan_three(back_two, r1_b, r2_b, o3_b, r3_b, 0, True)
+
     s1_low = inverse(collect(sent_s1_low, psh.at[1]))
     col_s[1, low] = col_of(s1_low)
     over_chunks(lambda where: gate_medium(where, low, col_s[1, low]))
     clear(low)
     clear(high)
     over_chunks(lambda where: medium_layer(where, high))
-    finish(back_three)
-
-    def back_long(rows, where, value):
-        spread = (local[rows, where] + value).astype(BF16).astype(F32)
-        u2[rows, where] = spread * pre[2, rows, where].astype(F32) * gains[2:3, where]
-
-    carried(r3_b, True, back_long)
-
-    def inner_sums(where, rows):
-        sums2[rows, :] += x2[rows, where].astype(F32) * u2[rows, where]
-
-    over_tiles(lambda where, t: inner_sums(where, high))
-    ps2[0, me] = jnp.concatenate([row_of(sums[high, :]), row_of(sums2[high, :])], axis=0)
-    sent_s2_high = exchange(ps2.at[0], 3)
-
+    scale_ahead.wait_recv()
+    col_h[...] = col_of(s1r[1])
     for q in range(chunks):
-        medium_halo[q].wait_recv()
+        stream_ahead[q].wait_recv()
+        value = x1h[:, part(q)].astype(F32) * twice(col_h[...])
+        a1[0:HALF, part(q)] = value.astype(BF16)
 
         @pl.when(k == 0)
         def _(q=q):
             a1[0:HALF, part(q)] = jnp.zeros((HALF, WIDE), BF16)
 
         medium_layer(part(q), low)
-        sums2[low, :] += fold(x2[low, part(q)].astype(F32) * u2[low, part(q)])
-    ps2[1, me] = jnp.concatenate([row_of(sums[low, :]), row_of(sums2[low, :])], axis=0)
-    sent_s2_low = exchange(ps2.at[1], 4)
+    finish(back_three)
+
+    def back_long(rows, where, value):
+        spread = (local[rows, where] + value).astype(BF16).astype(F32)
+        spread = spread * pre[2, rows, where].astype(F32) * gains[2:3, where]
+        u2[rows, where] = spread
+        sums2[rows, :] += x2[rows, where].astype(F32) * spread
+
+    carried(r3_b, True, back_long)
+    ps2[0, me] = jnp.concatenate([row_of(sums[low, :]), row_of(sums2[low, :])], axis=0)
+    sent_s2_low = exchange(ps2.at[0], 3)
+    ps2[1, me] = jnp.concatenate([row_of(sums[high, :]), row_of(sums2[high, :])], axis=0)
+    sent_s2_high = exchange(ps2.at[1], 4)
 
     def second_columns(sent, slots, rows):
         total = collect(sent, slots)
@@ -540,16 +547,6 @@
         g2[rows, where] = value
         e1[rows, where] = (post[1, rows, where].astype(F32) * value.astype(F32)).astype(BF16)
 
-    second_columns(sent_s2_low, ps2.at[1], low)
-    medium_back = []
-    for q in range(chunks):
-        back_two_rows(part(q), low)
-        medium_back.append(
-            halo(e1.at[pl.ds(0, HALF), part(q)], e1.at[pl.ds(ROWS, HALF), part(q)], 6 + q, preceding)
-        )
-    second_columns(sent_s2_high, ps2.at[0], high)
-    over_chunks(lambda where: back_two_rows(where, high))
-
     def gate_long(where, t):
         value = (
             pre[2, :, where].astype(F32)
@@ -559,9 +556,19 @@
         )
         a2[:, where] = value.astype(BF16)
 
-    over_tiles(gate_long)
-    states(a2, st_f, False)
-    fore_one = scan_one(st_f, r1_f, 1)
+    second_columns(sent_s2_low, ps2.at[0], low)
+    medium_back = []
+    for q in range(chunks):
+        back_two_rows(part(q), low)
+        medium_back.append(
+            halo(e1.at[pl.ds(0, HALF), part(q)], e1.at[pl.ds(ROWS, HALF), part(q)], 6 + q, preceding)
+        )
+        if q == 1:
+            second_columns(sent_s2_high, ps2.at[1], high)
+            over_tiles(gate_long)
+            states(a2, st_f, False)
+            fore_one = scan_one(st_f, r1_f, 1)
+    over_chunks(lambda where: back_two_rows(where, high))
 
     clear(low)
     clear(high)
@@ -637,7 +644,7 @@
         out[rows, where] = result.astype(BF16)
 
     carried(r3_f, False, fore_long)
-    store_out = pltpu.make_async_copy(out, out_h, store_sem.at[1])
+    store_out = pltpu.make_async_copy(out, both_h.at[0], store_sem.at[1])
     store_out.start()
 
     total = collect(sent_m0, ps0.at[1])
@@ -652,7 +659,7 @@
         grad[:, where] = value.astype(BF16)
 
     over_tiles(final_rows)
-    store_grad = pltpu.make_async_copy(grad, grad_h, store_sem.at[0])
+    store_grad = pltpu.make_async_copy(grad, both_h.at[1], store_sem.at[0])
     store_grad.start()
     for copy in leaving:
         copy.wait_send()
@@ -705,6 +712,10 @@
         vmem(whole, F32),
         vmem((WIDE, width), F32),
         vmem((2 * ROWS, width), F32),
+        vmem((HALF, width), BF16),
+        vmem((HALF, width), BF16),
+        vmem((2, 1, HALF), F32),
+        vmem((HALF, LANE), F32),
         vmem((ROWS, LANE), F32),
         vmem((ROWS, LANE), F32),
         vmem((3, ROWS, LANE), F32),
@@ -721,15 +732,15 @@
     ]
     sem = pltpu.SemaphoreType.DMA
     scratch += [
-        sem((17,)), sem((2,)), sem((8, tn)), sem((8, tn)), sem((10,)), sem((10,)),
+        sem((17,)), sem((2,)), sem((8, tn)), sem((8, tn)), sem((11,)), sem((11,)),
         sem((2, YN)), sem((2, YN)), sem((2, zn)), sem((2, zn)), sem((2, YN)), sem((2, YN)),
     ]
     any_spec = pl.BlockSpec(memory_space=pl.ANY)
-    return pl.pallas_call(
+    both = pl.pallas_call(
         functools.partial(kernel, zn, tn, channels),
-        out_shape=(jax.ShapeDtypeStruct(whole, BF16), jax.ShapeDtypeStruct(whole, BF16)),
+        out_shape=jax.ShapeDtypeStruct((2,) + whole, BF16),
         in_specs=[any_spec] * len(operands),
-        out_specs=(any_spec, any_spec),
+        out_specs=any_spec,
         scratch_shapes=scratch,
         compiler_params=pltpu.CompilerParams(
             collective_id=0, has_side_effects=True, vmem_limit_bytes=60 * 2**20
@@ -739,6 +750,7 @@
         ),
         name="hyena_group",
     )(*operands)
+    return both[0], both[1]
 
 
 def solution(mesh):

time: 60.5 us -> 56.2 us (0.929)
  Pallas kernels: 55.7 us -> 53.3 us
  local copies, waits for them, and re-layouts: 3.74 us -> 2.24 us
    unnamed x2 -> x0, local copies, waits for them, and re-layouts: 3.74 us -> none
    pallas_call x1, Pallas kernels: 55.7 us -> 53.3 us  [per_device(): pl.pallas_call(functools.partial(kernel, zn, tn, channels), out_shape=jax...]
    squeeze x0 -> x1, local copies, waits for them, and re-layouts: none -> 2.24 us  [per_device(): return (both[0], both[1])]
where the time goes in v3:
time: 56.2 us; the launch traced here: 56.1 us
  Pallas kernels  53.3 us (95%)
  local copies, waits for them, and re-layouts  2.24 us (4%)
  between operations  0.64 us (1%)
    pallas_call x1, Pallas kernels, per_device(): pl.pallas_call(functools.partial(kernel, zn, tn, channels), out_shape=jax...  53.3 us
    squeeze x1, local copies, waits for them, and re-layouts, per_device(): return (both[0], both[1])  2.24 us

profile of v3, /device:TPU:1, one launch (start us, length us, event | category | flops | bytes accessed | tf_op | source)
XLA Modules:
  0.0 56.1 jit_solution(3978089740724480445)
XLA Ops:
  0.6 53.3 %hyena_group.1 = bf16[2,256,1024]{2,1,0:T(8,128)(2,1)} custom-call(bf16[256,1024]{1,0:T(8,128)(2,1)} %stream_h.1, bf16[3,256,1024]{2,1,0:T(8,128)(2,1)} %pre_h.1, bf16[3,256,1024]{2,1,0:T(8,128)(2,1)} %post_h.1, f32[3,1024]{1,0:T(4,128)} %gains_h.1, f32[7,1024]{1,0:T(8,128)} %se_h.1, f32[128,1024]{1,0:T(8,128)} %mr_h.1, f32[16,1024]{1,0:T(8,128)} %bitcast.6, ...), custom_call_target="tpu_custom_call" | custom-call | flops 4000000000 | bytes 7000000 | tf_op jit(solution)/shard_map/hyena_group/pallas_call | solution.py:739
  53.9 2.2 %slice_bitcast_fusion = (bf16[256,1024]{1,0:T(8,128)(2,1)}, bf16[256,1024]{1,0:T(8,128)(2,1)}) fusion(bf16[2,256,1024]{2,1,0:T(8,128)(2,1)} %hyena_group.1), kind=kLoop, calls=%fused_computation | loop fusion | bytes 2097152 | tf_op jit(solution)/shard_map/squeeze | solution.py:753

commit v4 on v3

--- a/solution.py
+++ b/solution.py
@@ -414,9 +414,7 @@
     back_one = scan_one(st_b, r1_b, 0)
     for load in loads[5:]:
         load.wait()
-    filter_head()
     spectra(w1, mr, h1, HALF)
-    spectra(w2, taps, h2, ROWS)
     back_two = scan_two(back_one, r1_b, tz_b, r2_b, 0, True)
 
     s0 = inverse(collect(sent_s0, ps0.at[0]))
@@ -463,6 +461,8 @@
 
     over_tiles(lambda where, t: gate_stream(where, t, 0, 112))
     over_tiles(lambda where, t: short_layer(where, t, 16, 112))
+    filter_head()
+    spectra(w2, taps, h2, ROWS)
     short_halo.wait_recv()
 
     @pl.when(k == 0)
@@ -527,16 +527,8 @@
         sums2[rows, :] += x2[rows, where].astype(F32) * spread
 
     carried(r3_b, True, back_long)
-    ps2[0, me] = jnp.concatenate([row_of(sums[low, :]), row_of(sums2[low, :])], axis=0)
-    sent_s2_low = exchange(ps2.at[0], 3)
-    ps2[1, me] = jnp.concatenate([row_of(sums[high, :]), row_of(sums2[high, :])], axis=0)
-    sent_s2_high = exchange(ps2.at[1], 4)
-
-    def second_columns(sent, slots, rows):
-        total = collect(sent, slots)
-        s2 = inverse(total[0:1])
-        col_s[2, rows] = col_of(s2)
-        col_k[rows, :] = col_of(s2 * s2 * s2 * total[1:2] * (1.0 / channels))
+    ps2[me] = jnp.concatenate([row_of(sums[...]), row_of(sums2[...])], axis=0)
+    sent_s2 = exchange(ps2, 3)
 
     def back_two_rows(where, rows):
         value = (
@@ -556,7 +548,10 @@
         )
         a2[:, where] = value.astype(BF16)
 
-    second_columns(sent_s2_low, ps2.at[0], low)
+    total = collect(sent_s2, ps2)
+    s2 = inverse(total[0:1])
+    col_s[2] = col_of(s2)
+    col_k[...] = col_of(s2 * s2 * s2 * total[1:2] * (1.0 / channels))
     medium_back = []
     for q in range(chunks):
         back_two_rows(part(q), low)
@@ -564,7 +559,6 @@
             halo(e1.at[pl.ds(0, HALF), part(q)], e1.at[pl.ds(ROWS, HALF), part(q)], 6 + q, preceding)
         )
         if q == 1:
-            second_columns(sent_s2_high, ps2.at[1], high)
             over_tiles(gate_long)
             states(a2, st_f, False)
             fore_one = scan_one(st_f, r1_f, 1)
@@ -583,7 +577,6 @@
     over_chunks(lambda where: medium_adjoint(where, low))
     psh[2, me] = row_of(sums[low, :])
     sent_m1_low = exchange(psh.at[2], 5)
-    local_part(a2, False)
     fore_two = scan_two(fore_one, r1_f, tz_f, r2_f, 1, False)
 
     def back_one_rows(where, t, rows):
@@ -610,7 +603,6 @@
     col_k[low, :] = col_of(s1_low * s1_low * s1_low * total * (1.0 / channels))
     over_tiles(lambda where, t: back_one_rows(where, t, low))
     short_back = halo(e0.at[:, pl.ds(0, 8), :], e0.at[:, pl.ds(256, 8), :], 1, preceding)
-    over_tiles(lambda where, t: short_adjoint(where, t, 0, 112))
 
     for q in range(chunks):
         medium_back[q].wait_recv()
@@ -622,6 +614,8 @@
         medium_adjoint(part(q), high)
     psh[3, me] = row_of(sums[high, :])
     sent_m1_high = exchange(psh.at[3], 6)
+    over_tiles(lambda where, t: short_adjoint(where, t, 0, 112))
+    local_part(a2, False)
     fore_three = scan_three(fore_two, r1_f, r2_f, o3_f, r3_f, 1, False)
     short_back.wait_recv()
 
@@ -722,7 +716,7 @@
         vmem((ROWS, LANE), F32),
         vmem((2, tn, 1, ROWS), F32),
         vmem((4, tn, 1, HALF), F32),
-        vmem((2, tn, 2, HALF), F32),
+        vmem((tn, 2, ROWS), F32),
         vmem(scan, F32), vmem(scan, F32),
         vmem(scan, F32), vmem(scan, F32),
         vmem(scan[1:], F32), vmem(scan[1:], F32),

time: 56.2 us -> 55.8 us (level)
  no operation moved by 1% of the time
where the time goes in v4:
time: 55.8 us; the launch traced here: 55.7 us
  Pallas kernels  52.9 us (95%)
  local copies, waits for them, and re-layouts  2.24 us (4%)
  between operations  0.64 us (1%)
    pallas_call x1, Pallas kernels, per_device(): pl.pallas_call(functools.partial(kernel, zn, tn, channels), out_shape=jax...  52.9 us
    squeeze x1, local copies, waits for them, and re-layouts, per_device(): return (both[0], both[1])  2.24 us

profile of v4, /device:TPU:1, one launch (start us, length us, event | category | flops | bytes accessed | tf_op | source)
XLA Modules:
  0.0 55.7 jit_solution(18291320873635621823)
XLA Ops:
  0.6 52.9 %hyena_group.1 = bf16[2,256,1024]{2,1,0:T(8,128)(2,1)} custom-call(bf16[256,1024]{1,0:T(8,128)(2,1)} %stream_h.1, bf16[3,256,1024]{2,1,0:T(8,128)(2,1)} %pre_h.1, bf16[3,256,1024]{2,1,0:T(8,128)(2,1)} %post_h.1, f32[3,1024]{1,0:T(4,128)} %gains_h.1, f32[7,1024]{1,0:T(8,128)} %se_h.1, f32[128,1024]{1,0:T(8,128)} %mr_h.1, f32[16,1024]{1,0:T(8,128)} %bitcast.6, ...), custom_call_target="tpu_custom_call" | custom-call | flops 4000000000 | bytes 7000000 | tf_op jit(solution)/shard_map/hyena_group/pallas_call | solution.py:733
  53.5 2.2 %slice_bitcast_fusion = (bf16[256,1024]{1,0:T(8,128)(2,1)}, bf16[256,1024]{1,0:T(8,128)(2,1)}) fusion(bf16[2,256,1024]{2,1,0:T(8,128)(2,1)} %hyena_group.1), kind=kLoop, calls=%fused_computation | loop fusion | bytes 2097152 | tf_op jit(solution)/shard_map/squeeze | solution.py:747
